TPU v7x, 32 devices: a whole 2x2x4 slice. The times are simulated.
32 devices in a mesh: narrow: 4 (over z), wide: 8 (over y, x, core).
Axes of the slice: x: 2, y: 2, z: 4, core: 2. Of those that a mesh axis runs over, the one named last changes fastest.
Arguments:
- tokens: bfloat16 [16384, 1024], P('wide', 'narrow'), may hold values from -6 to 6
- condition: bfloat16 [16, 1024], P('wide'), may hold values from -6 to 6
- w_ada: bfloat16 [1024, 6, 1024], P('wide', None, 'narrow'), may hold values from -0.1875 to 0.1875
- b_ada: bfloat16 [6, 1024], P(None, ('narrow', 'wide')), may hold values from -3 to 3
- w_qkv: bfloat16 [1024, 3, 1024], P('wide', None, 'narrow'), may hold values from -0.1875 to 0.1875
- b_qv: bfloat16 [2, 1024], P(None, ('narrow', 'wide')), may hold values from -1.1953125 to 1.1953125
- w_proj: bfloat16 [1024, 1024], P('narrow', 'wide'), may hold values from -0.75 to 0.75
- b_proj: bfloat16 [1024], P(('narrow', 'wide')), may hold values from -3 to 3
- w_fc1: bfloat16 [1024, 4096], P('wide', 'narrow'), may hold values from -0.1875 to 0.1875
- b_fc1: bfloat16 [4096], P(('narrow', 'wide')), may hold values from -3 to 3
- w_fc2: bfloat16 [4096, 1024], P('narrow', 'wide'), may hold values from -0.09375 to 0.09375
- b_fc2: bfloat16 [1024], P(('narrow', 'wide')), may hold values from -3 to 3
- cotangent: bfloat16 [16384, 1024], P('wide', 'narrow'), may hold values from -6 to 6
Outputs:
- output: bfloat16 [16384, 1024], P('wide', 'narrow')
- grad_tokens: float32 [16384, 1024], P('wide', 'narrow')
- grad_cond: float32 [16, 1024], P('wide')
- grad_w_ada: float32 [1024, 6, 1024], P('wide', None, 'narrow')
- grad_b_ada: float32 [6, 1024], P(None, ('narrow', 'wide'))
- grad_w_qkv: float32 [1024, 3, 1024], P('wide', None, 'narrow')
- grad_b_qv: float32 [2, 1024], P(None, ('narrow', 'wide'))
- grad_w_proj: float32 [1024, 1024], P('narrow', 'wide')
- grad_b_proj: float32 [1024], P(('narrow', 'wide'))
- grad_w_fc1: float32 [1024, 4096], P('wide', 'narrow')
- grad_b_fc1: float32 [4096], P(('narrow', 'wide'))
- grad_w_fc2: float32 [4096, 1024], P('narrow', 'wide')
- grad_b_fc2: float32 [1024], P(('narrow', 'wide'))
All inputs are finite; a program needn't handle non-finite values.
Results may differ from a plain program's by a relative error of at most 0.019.
The roundings to bfloat16 on the way count: a program that leaves them out, or rounds other values in their place, can miss the bound.
Values may be sent and summed in bfloat16 or wider, within the bound.
A program may use at most 128 MiB of HBM per device.

v0:
```python
import jax
import jax.numpy as jnp
from jax import lax
from jax.sharding import PartitionSpec as P

HEADS = 16


norm_epsilon = 1e-06
gelu_factor = 0.7978845608028654
gelu_cubic = 0.044715


def gelu_tanh(values):
    return (
        0.5
        * values
        * (1.0 + jnp.tanh(gelu_factor * (values + gelu_cubic * values * values * values)))
    )


def gelu_slope(values):
    inner = jnp.tanh(gelu_factor * (values + gelu_cubic * values * values * values))
    return 0.5 * (1.0 + inner) + 0.5 * values * (1.0 - inner * inner) * gelu_factor * (
        1.0 + 3.0 * gelu_cubic * values * values
    )


def feature_totals(left_sum, right_sum):
    return lax.psum((left_sum, right_sum), "narrow")


def norm_forward(values, feature_count):
    sum_one, sum_two = feature_totals(jnp.sum(values, axis=1), jnp.sum(values * values, axis=1))
    row_mean = sum_one / feature_count
    row_var = sum_two / feature_count - row_mean * row_mean
    inverse = lax.rsqrt(row_var + norm_epsilon)
    return ((values - row_mean[:, None]) * inverse[:, None], inverse)


def norm_backward(grad_normed, normed, inverse, feature_count):
    sum_one, sum_two = feature_totals(
        jnp.sum(grad_normed, axis=1), jnp.sum(grad_normed * normed, axis=1)
    )
    return inverse[:, None] * (
        grad_normed - sum_one[:, None] / feature_count - normed * (sum_two[:, None] / feature_count)
    )


def gather_features(hidden):
    return lax.all_gather(hidden, "narrow", axis=1, tiled=True)


def branch_total(partial_value):
    rounded = lax.optimization_barrier(partial_value.astype(jnp.bfloat16)).astype(jnp.float32)
    return lax.psum_scatter(
        rounded.astype(jnp.bfloat16), "narrow", scatter_dimension=1, tiled=True
    ).astype(jnp.float32)


def gather_branch_grads(grad_part):
    return lax.all_gather(grad_part, "narrow", axis=1, tiled=True)


def feature_grads(partial_value):
    return lax.psum_scatter(
        partial_value.astype(jnp.bfloat16), "narrow", scatter_dimension=1, tiled=True
    ).astype(jnp.float32)


def fetch_blocks(w_qkv, w_proj, w_fc1, w_fc2, b_qv, b_proj, b_fc1, b_fc2, b_ada):
    return (
        lax.all_gather(w_qkv, "wide", axis=0, tiled=True),
        lax.all_gather(w_proj, "wide", axis=1, tiled=True),
        lax.all_gather(w_fc1, "wide", axis=0, tiled=True),
        lax.all_gather(w_fc2, "wide", axis=1, tiled=True),
        lax.all_gather(b_qv, "wide", axis=1, tiled=True),
        lax.all_gather(b_proj, "wide", axis=0, tiled=True),
        lax.all_gather(b_fc1, "wide", axis=0, tiled=True),
        lax.all_gather(b_fc2, "wide", axis=0, tiled=True),
        lax.all_gather(b_ada, "wide", axis=1, tiled=True),
    )


def per_device(
    tokens,
    condition,
    w_ada,
    b_ada,
    w_qkv,
    b_qv,
    w_proj,
    b_proj,
    w_fc1,
    b_fc1,
    w_fc2,
    b_fc2,
    cotangent,
):
    seq_count = condition.shape[0]
    row_count, part_width = tokens.shape
    length = row_count // seq_count
    feature_count = condition.shape[1]
    head_dim = feature_count // HEADS
    head_count = part_width // head_dim
    score_scale = head_dim ** (-0.5)

    def per_seq(values, rows_vec):
        return (values.reshape(seq_count, length, -1) * rows_vec[:, None, :]).reshape(row_count, -1)

    def seq_sums(values):
        return jnp.sum(values.reshape(seq_count, length, -1), axis=1)

    def modulate(normed, shift_rows, scale_rows):
        shaped = normed.reshape(seq_count, length, -1)
        return (shaped * (1.0 + scale_rows[:, None, :]) + shift_rows[:, None, :]).reshape(
            row_count, -1
        )

    def attend(seq_block):
        outputs = []
        lse_list = []
        for head_index in range(head_count):
            offset = head_index * head_dim
            query_rows = seq_block[:, 0, offset : offset + head_dim]
            key_rows = seq_block[:, 1, offset : offset + head_dim]
            value_rows = seq_block[:, 2, offset : offset + head_dim]
            scores = (
                jnp.einsum("qd,kd->qk", query_rows, key_rows, preferred_element_type=jnp.float32)
                * score_scale
            )
            row_top = jnp.max(scores, axis=1, keepdims=True)
            raised = jnp.exp(scores - row_top)
            row_total = jnp.sum(raised, axis=1, keepdims=True)
            soft_weights = (raised / row_total).astype(jnp.bfloat16)
            outputs.append(jnp.dot(soft_weights, value_rows, preferred_element_type=jnp.float32))
            lse_list.append(row_top[:, 0] + jnp.log(row_total[:, 0]))
        return (jnp.concatenate(outputs, axis=1), jnp.stack(lse_list))

    def attend_back(packed):
        seq_block, lse_rows, grad_block = packed
        pieces = []
        for head_index in range(head_count):
            offset = head_index * head_dim
            query_rows = seq_block[:, 0, offset : offset + head_dim]
            key_rows = seq_block[:, 1, offset : offset + head_dim]
            value_rows = seq_block[:, 2, offset : offset + head_dim]
            grad_head = grad_block[:, offset : offset + head_dim]
            scores = (
                jnp.einsum("qd,kd->qk", query_rows, key_rows, preferred_element_type=jnp.float32)
                * score_scale
            )
            soft_float = jnp.exp(scores - lse_rows[head_index][:, None])
            soft_weights = soft_float.astype(jnp.bfloat16)
            grad_value = jnp.einsum(
                "qk,qd->kd", soft_weights, grad_head, preferred_element_type=jnp.float32
            )
            grad_soft = jnp.einsum(
                "qd,kd->qk", grad_head, value_rows, preferred_element_type=jnp.float32
            )
            inner = jnp.sum(soft_float * grad_soft, axis=1, keepdims=True)
            grad_scores = (soft_float * (grad_soft - inner)).astype(jnp.bfloat16)
            grad_query = (
                jnp.dot(grad_scores, key_rows, preferred_element_type=jnp.float32) * score_scale
            )
            grad_key = (
                jnp.einsum("qk,qd->kd", grad_scores, query_rows, preferred_element_type=jnp.float32)
                * score_scale
            )
            pieces.append(jnp.stack([grad_query, grad_key, grad_value], axis=1))
        return jnp.concatenate(pieces, axis=2)

    inputs = tokens.astype(jnp.float32)
    cond_float = condition.astype(jnp.float32)
    cond_act = jax.nn.silu(cond_float).astype(jnp.bfloat16)
    qkv_full, proj_full, fc1_full, fc2_full, qv_bias, proj_bias, fc1_bias, fc2_bias, ada_bias = (
        fetch_blocks(w_qkv, w_proj, w_fc1, w_fc2, b_qv, b_proj, b_fc1, b_fc2, b_ada)
    )
    ada_full = lax.all_gather(w_ada, "wide", axis=0, tiled=True)
    modulation = jnp.dot(
        cond_act, ada_full.reshape(feature_count, -1), preferred_element_type=jnp.float32
    )
    modulation = modulation.reshape(seq_count, 6, part_width) + ada_bias.astype(jnp.float32)
    shift_one = modulation[:, 0]
    scale_one = modulation[:, 1]
    gate_one = modulation[:, 2]
    shift_two = modulation[:, 3]
    scale_two = modulation[:, 4]
    gate_two = modulation[:, 5]
    normed_one, inverse_one = norm_forward(inputs, feature_count)
    hidden_one = modulate(normed_one, shift_one, scale_one).astype(jnp.bfloat16)
    hidden_one_full = gather_features(hidden_one)
    qkv_bias = jnp.stack([qv_bias[0], jnp.zeros_like(qv_bias[0]), qv_bias[1]]).astype(jnp.float32)
    qkv_pre = jnp.dot(
        hidden_one_full, qkv_full.reshape(feature_count, -1), preferred_element_type=jnp.float32
    )
    qkv_low = (qkv_pre.reshape(row_count, 3, part_width) + qkv_bias).astype(jnp.bfloat16)
    qkv_seqs = qkv_low.reshape(seq_count, length, 3, part_width)
    attended, lse_all = lax.map(attend, qkv_seqs)
    attended_low = attended.reshape(row_count, part_width).astype(jnp.bfloat16)
    attn_branch = branch_total(
        jnp.dot(attended_low, proj_full, preferred_element_type=jnp.float32)
    ) + proj_bias.astype(jnp.float32)
    residual = inputs + per_seq(attn_branch, gate_one)
    normed_two, inverse_two = norm_forward(residual, feature_count)
    hidden_two = modulate(normed_two, shift_two, scale_two).astype(jnp.bfloat16)
    hidden_two_full = gather_features(hidden_two)
    pre_act = jnp.dot(
        hidden_two_full, fc1_full, preferred_element_type=jnp.float32
    ) + fc1_bias.astype(jnp.float32)
    activated = gelu_tanh(pre_act).astype(jnp.bfloat16)
    mlp_branch = branch_total(
        jnp.dot(activated, fc2_full, preferred_element_type=jnp.float32)
    ) + fc2_bias.astype(jnp.float32)
    output = residual + per_seq(mlp_branch, gate_two)
    grad_out = cotangent.astype(jnp.float32)
    (
        qkv_back,
        proj_back,
        fc1_back,
        fc2_back,
        qv_unused,
        proj_unused,
        fc1_unused,
        fc2_unused,
        ada_unused,
    ) = fetch_blocks(w_qkv, w_proj, w_fc1, w_fc2, b_qv, b_proj, b_fc1, b_fc2, b_ada)
    grad_gate_two = seq_sums(grad_out * mlp_branch)
    grad_mlp = per_seq(grad_out, gate_two).astype(jnp.bfloat16)
    grad_fc2_bias = jnp.sum(grad_mlp, axis=0, dtype=jnp.float32)
    grad_mlp_full = gather_branch_grads(grad_mlp)
    grad_fc2_part = jnp.einsum(
        "tf,td->fd", activated, grad_mlp_full, preferred_element_type=jnp.float32
    )
    grad_act = jnp.einsum("td,fd->tf", grad_mlp_full, fc2_back, preferred_element_type=jnp.float32)
    grad_pre = (grad_act * gelu_slope(pre_act)).astype(jnp.bfloat16)
    grad_fc1_bias = jnp.sum(grad_pre, axis=0, dtype=jnp.float32)
    grad_fc1_part = jnp.einsum(
        "td,tf->df", hidden_two_full, grad_pre, preferred_element_type=jnp.float32
    )
    grad_hidden_two = feature_grads(
        jnp.einsum("tf,df->td", grad_pre, fc1_back, preferred_element_type=jnp.float32)
    )
    grad_shift_two = seq_sums(grad_hidden_two)
    grad_scale_two = seq_sums(grad_hidden_two * normed_two)
    grad_residual = grad_out + norm_backward(
        per_seq(grad_hidden_two, 1.0 + scale_two), normed_two, inverse_two, feature_count
    )
    grad_gate_one = seq_sums(grad_residual * attn_branch)
    grad_attn = per_seq(grad_residual, gate_one).astype(jnp.bfloat16)
    grad_proj_bias = jnp.sum(grad_attn, axis=0, dtype=jnp.float32)
    grad_attn_full = gather_branch_grads(grad_attn)
    grad_proj_part = jnp.einsum(
        "th,td->hd", attended_low, grad_attn_full, preferred_element_type=jnp.float32
    )
    grad_attended = jnp.einsum(
        "td,hd->th", grad_attn_full, proj_back, preferred_element_type=jnp.float32
    ).astype(jnp.bfloat16)
    grad_qkv_seqs = lax.map(
        attend_back, (qkv_seqs, lse_all, grad_attended.reshape(seq_count, length, part_width))
    )
    grad_qkv = grad_qkv_seqs.reshape(row_count, 3, part_width).astype(jnp.bfloat16)
    qkv_sums = jnp.sum(grad_qkv, axis=0, dtype=jnp.float32)
    grad_qv_bias = jnp.stack([qkv_sums[0], qkv_sums[2]])
    grad_qkv_part = jnp.einsum(
        "td,tcn->dcn", hidden_one_full, grad_qkv, preferred_element_type=jnp.float32
    )
    grad_hidden_one = feature_grads(
        jnp.einsum("tcn,dcn->td", grad_qkv, qkv_back, preferred_element_type=jnp.float32)
    )
    grad_shift_one = seq_sums(grad_hidden_one)
    grad_scale_one = seq_sums(grad_hidden_one * normed_one)
    grad_inputs = grad_residual + norm_backward(
        per_seq(grad_hidden_one, 1.0 + scale_one), normed_one, inverse_one, feature_count
    )
    grad_mod = jnp.stack(
        [
            grad_shift_one,
            grad_scale_one,
            grad_gate_one,
            grad_shift_two,
            grad_scale_two,
            grad_gate_two,
        ],
        axis=1,
    ).astype(jnp.bfloat16)
    grad_ada_bias = jnp.sum(grad_mod, axis=0, dtype=jnp.float32)
    grad_ada_part = jnp.einsum(
        "sd,scn->dcn", cond_act, grad_mod, preferred_element_type=jnp.float32
    )
    grad_w_ada = lax.psum_scatter(grad_ada_part, "wide", scatter_dimension=0, tiled=True)
    cond_part = jnp.einsum("scn,dcn->sd", grad_mod, ada_full, preferred_element_type=jnp.float32)
    cond_total = lax.psum(cond_part, "narrow")
    sigmoid_cond = jax.nn.sigmoid(cond_float)
    grad_cond = cond_total * sigmoid_cond * (1.0 + cond_float * (1.0 - sigmoid_cond))
    (
        grad_w_qkv,
        grad_w_proj,
        grad_w_fc1,
        grad_w_fc2,
        grad_b_qv,
        grad_b_proj,
        grad_b_fc1,
        grad_b_fc2,
        grad_b_ada,
    ) = (
        lax.psum_scatter(grad_qkv_part, "wide", scatter_dimension=0, tiled=True),
        lax.psum_scatter(grad_proj_part, "wide", scatter_dimension=1, tiled=True),
        lax.psum_scatter(grad_fc1_part, "wide", scatter_dimension=0, tiled=True),
        lax.psum_scatter(grad_fc2_part, "wide", scatter_dimension=1, tiled=True),
        lax.psum_scatter(grad_qv_bias, "wide", scatter_dimension=1, tiled=True),
        lax.psum_scatter(grad_proj_bias, "wide", scatter_dimension=0, tiled=True),
        lax.psum_scatter(grad_fc1_bias, "wide", scatter_dimension=0, tiled=True),
        lax.psum_scatter(grad_fc2_bias, "wide", scatter_dimension=0, tiled=True),
        lax.psum_scatter(grad_ada_bias, "wide", scatter_dimension=1, tiled=True),
    )
    return (
        output.astype(jnp.bfloat16),
        grad_inputs,
        grad_cond,
        grad_w_ada,
        grad_b_ada,
        grad_w_qkv,
        grad_b_qv,
        grad_w_proj,
        grad_b_proj,
        grad_w_fc1,
        grad_b_fc1,
        grad_w_fc2,
        grad_b_fc2,
    )


def solution(mesh):
    return jax.shard_map(
        per_device,
        mesh=mesh,
        in_specs=(
            P("wide", "narrow"),
            P("wide", None),
            P("wide", None, "narrow"),
            P(None, ("narrow", "wide")),
            P("wide", None, "narrow"),
            P(None, ("narrow", "wide")),
            P("narrow", "wide"),
            P(("narrow", "wide")),
            P("wide", "narrow"),
            P(("narrow", "wide")),
            P("narrow", "wide"),
            P(("narrow", "wide")),
            P("wide", "narrow"),
        ),
        out_specs=(
            P("wide", "narrow"),
            P("wide", "narrow"),
            P("wide", None),
            P("wide", None, "narrow"),
            P(None, ("narrow", "wide")),
            P("wide", None, "narrow"),
            P(None, ("narrow", "wide")),
            P("narrow", "wide"),
            P(("narrow", "wide")),
            P("wide", "narrow"),
            P(("narrow", "wide")),
            P("narrow", "wide"),
            P(("narrow", "wide")),
        ),
        check_vma=False,
    )
```

profile of v0, /device:TPU:0, one launch (start us, length us, event | category | flops | bytes accessed | tf_op | source)
XLA Modules:
  0.0 1243.3 jit_solution(17363905217399980786)
XLA Ops:
  8.7 10.5 all-gather
  19.3 1.9 convert_reduce_fusion.2
  21.2 19.0 %all-reduce.9 = (f32[2048]{0:T(1024)S(1)}, f32[2048]{0:T(1024)S(1)}) all-reduce(f32[2048]{0:T(1024)S(1)} %get-tuple-element.114, f32[2048]{0:T(1024)S(1)} %get-tuple-element.113), channel_id=1, replica_groups=mesh['narrow'=4,'wide'=8] {'narrow'}, use_global_device_ids=true, to_apply=%region_3.4 | all-reduce | flops 4096 | bytes 32768 | tf_op jit(solution)/shard_map/psum | solution.py:30
  40.2 4.7 all-gather.12.cloned.1.call-done
  45.0 3.2 copy.47
  49.8 1.5 fusion.85
  51.4 8.7 all-gather.1
  60.3 11.5 all_gather.51
  71.8 2.2 all-gather.16.cloned.1.call-done
  74.0 2.6 copy.49
  76.6 80.2 %all-gather.14.cloned.1.call-done = bf16[2048,1024]{1,0:T(8,128)(2,1)} async-done(((bf16[2048,256]{1,0:T(8,128)(2,1)}), bf16[2048,1024]{1,0:T(8,128)(2,1)}) %all-gather.14.cloned.1.call-update) | async-done | bytes 4194320 | tf_op jit(solution)/shard_map/all_gather | solution.py:51
  156.8 6.2 add_convert_fusion
  163.0 3.1 copy.51
  166.0 25.9 %while.22 = (s32[]{:T(128)}, bf16[2,1024,256]{2,1,0:T(8,128)(2,1)}, f32[2,4,1024]{2,1,0:T(4,128)S(1)}, bf16[2,1024,3,256]{1,3,2,0:T(8,128)(2,1)}, s32[]{:T(128)}) while((s32[]{:T(128)}, bf16[2,1024,256]{2,1,0:T(8,128)(2,1)}, f32[2,4,1024]{2,1,0:T(4,128)S(1)}, bf16[2,1024,3,256]{1,3,2,0:T(8,128)(2,1)}, s32[]{:T(128)}) %tuple.96), condition=%wide.region_13.14_spmd, body=%wide.region_4.13_spmd.sunk | while | flops 1113595904 | bytes 67272832 | solution.py:199
  166.5 1.5 dynamic-slice_bitcast_fusion.6
  179.2 1.5 dynamic-slice_bitcast_fusion.6
  191.9 4.4 convolution_convert_fusion
  198.8 14.1 %all-reduce.10 = (bf16[256]{0:T(256)(128)(2,1)S(1)}, bf16[256]{0:T(256)(128)(2,1)S(1)}) all-reduce(bf16[256]{0:T(256)(128)(2,1)S(1)} %dynamic-update-slice, bf16[256]{0:T(256)(128)(2,1)S(1)} %dynamic-update-slice.1), channel_id=1, replica_groups=mesh['narrow'=4,'wide'=8] {'wide'}, use_global_device_ids=true, to_apply=%add | all-reduce | flops 512 | bytes 2048
  212.9 58.6 %reduce-scatter.16.cloned.1.call-done = bf16[2048,256]{1,0:T(8,128)(2,1)} async-done(((bf16[2048,1024]{1,0:T(8,128)(2,1)}), bf16[2048,256]{1,0:T(8,128)(2,1)}) %reduce-scatter.16.cloned.1.call-update) | async-done | bytes 1048592 | tf_op jit(solution)/shard_map/reduce_scatter | solution.py:56
  271.5 2.1 fusion.122
  273.6 18.0 %all-reduce.8 = (f32[2048]{0:T(1024)S(1)}, f32[2048]{0:T(1024)S(1)}) all-reduce(f32[2048]{0:T(1024)S(1)} %get-tuple-element.103, f32[2048]{0:T(1024)S(1)} %get-tuple-element.102), channel_id=1, replica_groups=mesh['narrow'=4,'wide'=8] {'narrow'}, use_global_device_ids=true, to_apply=%region_18.19 | all-reduce | flops 4096 | bytes 32768 | tf_op jit(solution)/shard_map/psum | solution.py:30
  291.6 2.6 fusion.88
  295.1 1.9 convert_reduce_fusion.3
  297.0 8.9 all-gather.2
  306.0 78.5 %all-gather.18.cloned.1.call-done = bf16[2048,1024]{1,0:T(8,128)(2,1)} async-done(((bf16[2048,256]{1,0:T(8,128)(2,1)}), bf16[2048,1024]{1,0:T(8,128)(2,1)}) %all-gather.18.cloned.1.call-update) | async-done | bytes 4194320 | tf_op jit(solution)/shard_map/all_gather | solution.py:51
  384.5 10.6 fusion.129
  395.1 17.8 %all-gather.22.cloned.1.call-done = bf16[1024,1024]{1,0:T(8,128)(2,1)} async-done(((bf16[1024,128]{1,0:T(8,128)(2,1)}), bf16[1024,1024]{1,0:T(8,128)(2,1)}) %all-gather.22.cloned.1.call-update) | async-done | bytes 2097168 | tf_op jit(solution)/shard_map/all_gather | solution.py:76
  412.9 82.8 %all-gather.24.cloned.1.call-done = bf16[2048,1024]{1,0:T(8,128)(2,1)} async-done(((bf16[2048,256]{1,0:T(8,128)(2,1)}), bf16[2048,1024]{1,0:T(8,128)(2,1)}) %all-gather.24.cloned.1.call-update) | async-done | bytes 4194320 | tf_op jit(solution)/shard_map/all_gather | solution.py:62
  495.7 13.9 %convert_reduce_fusion = (f32[1024]{0:T(1024)}, bf16[2048,1024]{1,0:T(8,128)(2,1)S(1)}) fusion(f32[2048,1024]{1,0:T(8,128)} %fusion.129, f32[1024]{0:T(1024)S(1)} %bitcast.497, bf16[2048,1024]{1,0:T(8,128)(2,1)} %all-gather.24.cloned.1.call-done, bf16[1024,1024]{1,0:T(8,128)(2,1)} %all-gather.22.cloned.1.call-done), kind=kOutput, calls=%fused_computation.139 | convolution fusion | flops 4341103616 | bytes 18882560 | tf_op jit(solution)/shard_map/td,fd->tf/dot_general | solution.py:235
  509.7 1.9 copy-done.48
  511.6 6.3 convolution_convert_fusion.1
  518.3 11.8 convolution_convert_fusion.2
  530.3 62.7 %reduce-scatter.20.cloned.1.call-done = bf16[2048,256]{1,0:T(8,128)(2,1)} async-done(((bf16[2048,1024]{1,0:T(8,128)(2,1)}), bf16[2048,256]{1,0:T(8,128)(2,1)}) %reduce-scatter.20.cloned.1.call-update) | async-done | bytes 1048592 | tf_op jit(solution)/shard_map/reduce_scatter | solution.py:66
  593.0 2.7 fusion.103
  595.6 18.4 %all-reduce.7 = (f32[2048]{0:T(1024)S(1)}, f32[2048]{0:T(1024)S(1)}) all-reduce(f32[2048]{0:T(1024)S(1)} %get-tuple-element.107, f32[2048]{0:T(1024)S(1)} %get-tuple-element.106), channel_id=1, replica_groups=mesh['narrow'=4,'wide'=8] {'narrow'}, use_global_device_ids=true, to_apply=%region_24.25 | all-reduce | flops 4096 | bytes 32768 | tf_op jit(solution)/shard_map/psum | solution.py:30
  614.1 58.7 %reduce-scatter.18.cloned.1.call-done = bf16[2048,256]{1,0:T(8,128)(2,1)} async-done(((bf16[2048,1024]{1,0:T(8,128)(2,1)}), bf16[2048,256]{1,0:T(8,128)(2,1)}) %reduce-scatter.18.cloned.1.call-update) | async-done | bytes 1048592 | tf_op jit(solution)/shard_map/reduce_scatter | solution.py:56
  672.7 5.5 convert_reduce_fusion.4
  678.3 81.1 %all-gather.26.cloned.1.call-done = bf16[2048,1024]{1,0:T(8,128)(2,1)} async-done(((bf16[2048,256]{1,0:T(8,128)(2,1)}), bf16[2048,1024]{1,0:T(8,128)(2,1)}) %all-gather.26.cloned.1.call-update) | async-done | bytes 4194320 | tf_op jit(solution)/shard_map/all_gather | solution.py:62
  759.4 3.6 convolution_convert_fusion.3
  763.0 50.8 %while.23 = (s32[]{:T(128)}, bf16[2,1024,3,256]{3,1,0,2:T(8,128)(2,1)}, bf16[2,1024,3,256]{1,3,2,0:T(8,128)(2,1)}, f32[2,4,1024]{2,1,0:T(4,128)S(1)}, bf16[2,102...) while((s32[]{:T(128)}, bf16[2,1024,3,256]{3,1,0,2:T(8,128)(2,1)}, ...), condition=%wide.region_30.31_spmd, body=%wide.region_25.0_spmd.sunk | while | flops 2754605056 | bytes 154255584 | solution.py:259
  763.3 1.8 dynamic-slice_bitcast_fusion.7
  788.3 1.8 dynamic-slice_bitcast_fusion.7
  813.7 7.8 bitcast_convert_fusion
  822.7 1.6 bitcast_reduce_fusion
  824.3 3.0 convert_reduce_fusion.1
  828.2 68.5 %reduce-scatter.22.cloned.1.call-done = bf16[2048,256]{1,0:T(8,128)(2,1)} async-done(((bf16[2048,1024]{1,0:T(8,128)(2,1)}), bf16[2048,256]{1,0:T(8,128)(2,1)}) %reduce-scatter.22.cloned.1.call-update) | async-done | bytes 1048592 | tf_op jit(solution)/shard_map/reduce_scatter | solution.py:66
  896.7 3.6 bitcast_reduce_fusion.1
  901.3 12.5 %fusion.123 = f32[1024,1024]{1,0:T(8,128)} fusion(bf16[2048,1024]{1,0:T(8,128)(2,1)} %all-gather.24.cloned.1.call-done, f32[2048,1024]{1,0:T(8,128)} %fusion.129, f32[1024]{0:T(1024)S(1)} %bitcast.499), kind=kOutput, calls=%fused_computation.242 | convolution fusion | flops 4315938816 | bytes 16781312 | tf_op jit(solution)/shard_map/tf,td->fd/dot_general | solution.py:232
  914.0 10.0 fusion.131
  925.2 4.5 fusion.130
  929.8 8.4 fusion.76
  938.9 3.7 fusion.117
  944.1 14.0 %all-reduce.5 = (f32[256]{0:T(256)S(1)}, f32[1024]{0:T(1024)S(1)}, f32[256]{0:T(256)S(1)}) all-reduce(f32[256]{0:T(256)S(1)} %copy-done.38, f32[1024]{0:T(1024)S(1)} %copy-done.39, f32[256]{0:T(256)S(1)} %copy-done.37), channel_id=11, replica_groups=mesh['narrow'=4,'wide'=8] {'wide'}, use_global_device_ids=true, to_apply=%region_51.52.clone | all-reduce | flops 1536 | bytes 12288
  959.8 1.4 copy.61
  961.2 2.3 fusion.102
  963.5 2.8 convolution_bitcast_fusion
  966.3 18.4 %all-reduce.6 = (f32[2048]{0:T(1024)S(1)}, f32[2048]{0:T(1024)S(1)}, f32[2,1024]{1,0:T(2,128)S(1)}) all-reduce(f32[2048]{0:T(1024)S(1)} %get-tuple-element.105, f32[2048]{0:T(1024)S(1)} %get-tuple-element.104, f32[2,1024]{1,0:T(2,128)S(1)} %convolution_bitcast_fusion), channel_id=1, replica_groups=mesh['narrow'=4,'wide'=8] {'narrow'}, use_global_device_ids=true, to_apply=%region_35.36 | all-reduce | flops 6144 | bytes 49152 | tf_op jit(solution)/shard_map/psum | solution.py:30
  984.7 3.3 fusion.99
  988.7 1.4 copy.59
  990.0 35.2 %reduce-scatter.32.cloned.1.call-done = f32[1024,128]{1,0:T(8,128)} async-done(((f32[1024,1024]{1,0:T(8,128)}), f32[1024,128]{1,0:T(8,128)}) %reduce-scatter.32.cloned.1.call-update) | async-done | bytes 524304 | tf_op jit(solution)/shard_map/reduce_scatter | solution.py:310
  1025.2 55.5 %reduce-scatter.30.cloned.1.call-done = f32[128,1024]{1,0:T(8,128)} async-done(((f32[1024,1024]{1,0:T(8,128)}), f32[128,1024]{1,0:T(8,128)}) %reduce-scatter.30.cloned.1.call-update) | async-done | bytes 524304 | tf_op jit(solution)/shard_map/reduce_scatter | solution.py:309
  1080.8 39.6 %reduce-scatter.28.cloned.1.call-done = f32[256,128]{1,0:T(8,128)} async-done(((f32[256,1024]{1,0:T(8,128)}), f32[256,128]{1,0:T(8,128)}) %reduce-scatter.28.cloned.1.call-update) | async-done | bytes 131088 | tf_op jit(solution)/shard_map/reduce_scatter | solution.py:308
  1120.4 50.1 %reduce-scatter.26.cloned.1.call-done = f32[128,3,256]{2,0,1:T(8,128)} async-done(((f32[1024,3,256]{2,0,1:T(8,128)}), f32[128,3,256]{2,0,1:T(8,128)}) %reduce-scatter.26.cloned.1.call-update) | async-done | bytes 393232 | tf_op jit(solution)/shard_map/reduce_scatter | solution.py:307
  1170.5 66.1 %reduce-scatter.24.cloned.1.call-done = f32[128,6,256]{2,0,1:T(8,128)} async-done(((f32[1024,6,256]{2,0,1:T(8,128)}), f32[128,6,256]{2,0,1:T(8,128)}) %reduce-scatter.24.cloned.1.call-update) | async-done | bytes 786448 | tf_op jit(solution)/shard_map/reduce_scatter | solution.py:291
  (284 shorter events, 82.6 us)
Async XLA Ops:
  7.2 37.8 %all-gather.12.cloned.1.call-start = ((), (), s32[]{:S(2)}) async-start(), calls=%async_computation.11 | async-start | bytes 3538944 | tf_op jit(solution)/shard_map/all_gather | solution.py:179
  7.9 66.1 %all-gather.16.cloned.1.call-start = ((), (), s32[]{:S(2)}) async-start(), calls=%async_computation.13 | async-start | bytes 1769472 | tf_op jit(solution)/shard_map/all_gather | solution.py:73
  8.7 148.1 %all-gather.14.cloned.1.call-start = ((), (), s32[]{:S(2)}) async-start(), calls=%async_computation.12 | async-start | bytes 5242880 | tf_op jit(solution)/shard_map/all_gather | solution.py:51
  40.2 9.5 copy-start.15
  40.2 9.5 copy-start.17
  40.2 7.9 copy-start.26
  48.2 1.6 copy-start
  48.2 3.2 copy-start.43
  48.2 12.1 copy-start.25
  49.7 1.6 copy-start.28
  51.3 220.2 %reduce-scatter.16.cloned.1.call-start = ((), (), s32[]{:S(2)}) async-start(), calls=%async_computation.14 | async-start | bytes 5242880 | tf_op jit(solution)/shard_map/reduce_scatter | solution.py:56
  166.0 25.9 %copy-start.14 = (bf16[256,1024]{1,0:T(8,128)(2,1)S(1)}, bf16[256,1024]{1,0:T(8,128)(2,1)}, u32[]{:S(2)}) copy-start(bf16[256,1024]{1,0:T(8,128)(2,1)} %all_gather.51) | copy-start | bytes 1572868
  176.9 1.3 copy-start.11
  196.3 2.0 copy-start.46
  196.3 2.2 copy-start.47
  196.3 75.2 %copy-start.1 = (bf16[2048,256]{1,0:T(8,128)(2,1)S(1)}, bf16[2048,256]{1,0:T(8,128)(2,1)}, u32[]{:S(2)}) copy-start(bf16[2048,256]{1,0:T(8,128)(2,1)} %param.17) | copy-start | bytes 3145732
  196.3 75.2 %copy-start.23 = (f32[2,256]{1,0:T(2,128)S(1)}, f32[2,256]{1,0:T(2,128)}, u32[]{:S(2)}) copy-start(f32[2,256]{1,0:T(2,128)} %get-tuple-element.176) | copy-start | bytes 6148
  196.3 95.3 %copy-start.30 = (f32[2,256]{1,0:T(2,128)S(1)}, f32[2,256]{1,0:T(2,128)}, u32[]{:S(2)}) copy-start(f32[2,256]{1,0:T(2,128)} %get-tuple-element.175) | copy-start | bytes 6148
  196.3 95.3 %copy-start.34 = (f32[2,256]{1,0:T(2,128)S(1)}, f32[2,256]{1,0:T(2,128)}, u32[]{:S(2)}) copy-start(f32[2,256]{1,0:T(2,128)} %get-tuple-element.174) | copy-start | bytes 6148
  196.4 109.6 %all-gather.20.cloned.1.call-start = ((), (), s32[]{:S(2)}) async-start(), calls=%async_computation.16 | async-start | bytes 2359296 | tf_op jit(solution)/shard_map/all_gather | solution.py:75
  197.0 187.5 %all-gather.18.cloned.1.call-start = ((), (), s32[]{:S(2)}) async-start(), calls=%async_computation.15 | async-start | bytes 5242880 | tf_op jit(solution)/shard_map/all_gather | solution.py:51
  212.9 459.9 %copy-start.31 = (f32[256]{0:T(256)}, f32[256]{0:T(256)S(1)}, u32[]{:S(2)}) copy-start(f32[256]{0:T(256)S(1)} %convert_element_type.163) | copy-start | bytes 3076
  271.5 23.6 %copy-start.6 = (bf16[2048,256]{1,0:T(8,128)(2,1)S(1)}, bf16[2048,256]{1,0:T(8,128)(2,1)}, u32[]{:S(2)}) copy-start(bf16[2048,256]{1,0:T(8,128)(2,1)} %param.29) | copy-start | bytes 3145732
  271.5 23.6 %copy-start.33 = (f32[2,256]{1,0:T(2,128)S(1)}, f32[2,256]{1,0:T(2,128)}, u32[]{:S(2)}) copy-start(f32[2,256]{1,0:T(2,128)} %get-tuple-element.173) | copy-start | bytes 6148
  291.6 381.2 %copy-start.19 = (f32[2048]{0:T(1024)}, f32[2048]{0:T(1024)S(1)}, u32[]{:S(2)}) copy-start(f32[2048]{0:T(1024)S(1)} %get-tuple-element.179) | copy-start | bytes 24580
  291.6 381.2 %copy-start.21 = (f32[2048]{0:T(1024)}, f32[2048]{0:T(1024)S(1)}, u32[]{:S(2)}) copy-start(f32[2048]{0:T(1024)S(1)} %get-tuple-element.180) | copy-start | bytes 24580
  291.6 5.4 copy-start.44
  294.3 118.7 %all-gather.22.cloned.1.call-start = ((), (), s32[]{:S(2)}) async-start(), calls=%async_computation.17 | async-start | bytes 2359296 | tf_op jit(solution)/shard_map/all_gather | solution.py:76
  295.0 200.7 %all-gather.24.cloned.1.call-start = ((), (), s32[]{:S(2)}) async-start(), calls=%async_computation.19 | async-start | bytes 5242880 | tf_op jit(solution)/shard_map/all_gather | solution.py:62
  297.0 296.0 %reduce-scatter.20.cloned.1.call-start = ((), (), s32[]{:S(2)}) async-start(), calls=%async_computation.20 | async-start | bytes 5242880 | tf_op jit(solution)/shard_map/reduce_scatter | solution.py:66
  305.9 212.4 %copy-start.40 = (f32[8,1,128]{2,1,0:T(1,128)}, f32[8,1,128]{2,1,0:T(1,128)S(1)}, u32[]{:S(2)}) copy-start(f32[8,1,128]{2,1,0:T(1,128)S(1)} %convert_element_type.188) | copy-start | bytes 12292
  495.7 15.8 %copy-start.45 = (bf16[1024,1024]{1,0:T(8,128)(2,1)S(1)}, bf16[1024,1024]{1,0:T(8,128)(2,1)}, u32[]{:S(2)}) copy-start(bf16[1024,1024]{1,0:T(8,128)(2,1)} %all-gather.20.cloned.1.call-done) | copy-start | bytes 6291460
  509.7 1.9 copy-start.48
  517.9 154.9 %reduce-scatter.18.cloned.1.call-start = ((), (), s32[]{:S(2)}) async-start(), calls=%async_computation.18 | async-start | bytes 5242880 | tf_op jit(solution)/shard_map/reduce_scatter | solution.py:56
  530.2 62.8 %copy-start.3 = (bf16[2048,256]{1,0:T(8,128)(2,1)S(1)}, bf16[2048,256]{1,0:T(8,128)(2,1)}, u32[]{:S(2)}) copy-start(bf16[2048,256]{1,0:T(8,128)(2,1)} %reduce-scatter.16.cloned.1.call-done) | copy-start | bytes 3145732
  530.2 229.2 %all-gather.26.cloned.1.call-start = ((), (), s32[]{:S(2)}) async-start(), calls=%async_computation.21 | async-start | bytes 5242880 | tf_op jit(solution)/shard_map/all_gather | solution.py:62
  530.3 148.0 %copy-start.35 = (f32[256]{0:T(256)}, f32[256]{0:T(256)S(1)}, u32[]{:S(2)}) copy-start(f32[256]{0:T(256)S(1)} %convert_element_type.169) | copy-start | bytes 3076
  678.3 218.4 %reduce-scatter.22.cloned.1.call-start = ((), (), s32[]{:S(2)}) async-start(), calls=%async_computation.22 | async-start | bytes 5242880 | tf_op jit(solution)/shard_map/reduce_scatter | solution.py:66
  763.2 2.7 copy-start.9
  786.6 1.7 copy-start.10
  788.3 2.7 copy-start.9
  811.7 1.7 copy-start.10
  821.5 75.1 %copy-start.2 = (bf16[2048,256]{1,0:T(8,128)(2,1)S(1)}, bf16[2048,256]{1,0:T(8,128)(2,1)}, u32[]{:S(2)}) copy-start(bf16[2048,256]{1,0:T(8,128)(2,1)} %param.17) | copy-start | bytes 3145732
  821.5 75.1 %copy-start.4 = (bf16[2048,256]{1,0:T(8,128)(2,1)S(1)}, bf16[2048,256]{1,0:T(8,128)(2,1)}, u32[]{:S(2)}) copy-start(bf16[2048,256]{1,0:T(8,128)(2,1)} %reduce-scatter.16.cloned.1.call-done) | copy-start | bytes 3145732
  821.6 75.1 %copy-start.16 = (f32[2048]{0:T(1024)S(1)}, f32[2048]{0:T(1024)}, u32[]{:S(2)}) copy-start(f32[2048]{0:T(1024)} %copy-done.15) | copy-start | bytes 24580
  821.6 75.1 %copy-start.18 = (f32[2048]{0:T(1024)S(1)}, f32[2048]{0:T(1024)}, u32[]{:S(2)}) copy-start(f32[2048]{0:T(1024)} %copy-done.17) | copy-start | bytes 24580
  821.6 75.1 %copy-start.20 = (f32[2048]{0:T(1024)S(1)}, f32[2048]{0:T(1024)}, u32[]{:S(2)}) copy-start(f32[2048]{0:T(1024)} %copy-done.19) | copy-start | bytes 24580
  821.6 75.1 %copy-start.22 = (f32[2048]{0:T(1024)S(1)}, f32[2048]{0:T(1024)}, u32[]{:S(2)}) copy-start(f32[2048]{0:T(1024)} %copy-done.21) | copy-start | bytes 24580
  821.6 75.1 %copy-start.24 = (f32[2,256]{1,0:T(2,128)S(1)}, f32[2,256]{1,0:T(2,128)}, u32[]{:S(2)}) copy-start(f32[2,256]{1,0:T(2,128)} %get-tuple-element.176) | copy-start | bytes 6148
  821.6 75.1 %copy-start.32 = (f32[256]{0:T(256)S(1)}, f32[256]{0:T(256)}, u32[]{:S(2)}) copy-start(f32[256]{0:T(256)} %copy-done.31) | copy-start | bytes 3076
  821.6 138.2 %reduce-scatter.36.cloned.1.call-start = ((), (), s32[]{:S(2)}) async-start(), calls=%async_computation.29 | async-start | bytes 147456
  824.3 72.4 %copy-start.8 = (bf16[2048,256]{1,0:T(8,128)(2,1)S(1)}, bf16[2048,256]{1,0:T(8,128)(2,1)}, u32[]{:S(2)}) copy-start(bf16[2048,256]{1,0:T(8,128)(2,1)} %reduce-scatter.20.cloned.1.call-done) | copy-start | bytes 3145732
  828.1 160.5 %reduce-scatter.34.cloned.1.call-start = ((), (), s32[]{:S(2)}) async-start(), calls=%async_computation.28 | async-start | bytes 147456
  896.7 4.6 copy-start.41
  901.2 124.0 %reduce-scatter.32.cloned.1.call-start = ((), (), s32[]{:S(2)}) async-start(), calls=%async_computation.27 | async-start | bytes 4718592 | tf_op jit(solution)/shard_map/reduce_scatter | solution.py:310
  913.8 167.0 %reduce-scatter.30.cloned.1.call-start = ((), (), s32[]{:S(2)}) async-start(), calls=%async_computation.26 | async-start | bytes 4718592 | tf_op jit(solution)/shard_map/reduce_scatter | solution.py:309
  924.0 196.4 %reduce-scatter.28.cloned.1.call-start = ((), (), s32[]{:S(2)}) async-start(), calls=%async_computation.25 | async-start | bytes 1179648 | tf_op jit(solution)/shard_map/reduce_scatter | solution.py:308
  929.7 240.8 %reduce-scatter.26.cloned.1.call-start = ((), (), s32[]{:S(2)}) async-start(), calls=%async_computation.24 | async-start | bytes 3538944 | tf_op jit(solution)/shard_map/reduce_scatter | solution.py:307
  938.2 298.3 %reduce-scatter.24.cloned.1.call-start = ((), (), s32[]{:S(2)}) async-start(), calls=%async_computation.23 | async-start | bytes 7077888 | tf_op jit(solution)/shard_map/reduce_scatter | solution.py:291
  942.6 1.5 copy-start.37
  942.6 1.5 copy-start.38
  942.6 1.5 copy-start.39
  942.6 18.6 %copy-start.29 = (f32[2,256]{1,0:T(2,128)S(1)}, f32[2,256]{1,0:T(2,128)}, u32[]{:S(2)}) copy-start(f32[2,256]{1,0:T(2,128)} %copy-done.28) | copy-start | bytes 6148
  942.6 42.1 %copy-start.5 = (f32[2048,256]{1,0:T(8,128)S(1)}, f32[2048,256]{1,0:T(8,128)}, u32[]{:S(2)}) copy-start(f32[2048,256]{1,0:T(8,128)} %get-tuple-element.151) | copy-start | bytes 6291460
  (8 other events, 8.3 us)
Sparse Core Ops, SparseCore 0:
  9.9 35.0 all-gather.11
  46.9 27.1 all-gather.15
  76.2 80.5 all-gather.13
  196.5 74.9 reduce-scatter.15
  273.4 28.3 all-gather.19
  303.9 80.5 all-gather.17
  386.5 26.3 all-gather.21
  415.1 80.5 all-gather.23
  518.0 74.9 reduce-scatter.19
  595.1 77.5 reduce-scatter.17
  678.4 80.9 all-gather.25
  821.7 74.9 reduce-scatter.21
  899.6 33.8 reduce-scatter.35
  936.6 33.3 reduce-scatter.33
  973.8 51.3 reduce-scatter.31
  1029.4 51.3 reduce-scatter.29
  1084.4 35.9 reduce-scatter.27
  1124.2 46.2 reduce-scatter.25
  1174.8 61.7 reduce-scatter.23
where the time goes:
time: 1250 us; the launch traced here: 1240 us
  waiting for transfers between devices  845 us (68%)
  matrix products  153 us (12%)
  blocking collectives  141 us (11%)
  other arithmetic  49 us (4%)
  local copies, waits for them, and re-layouts  35.3 us (3%)
  between operations  16.9 us (1%)
    all_gather x2, waiting for transfers between devices, gather_branch_grads(): return lax.all_gather(grad_part, 'narrow', axis=1, tiled=True)  164 us
    all_gather x2, waiting for transfers between devices, gather_features(): return lax.all_gather(hidden, 'narrow', axis=1, tiled=True)  159 us
    reduce_scatter x2, waiting for transfers between devices, feature_grads(): lax.psum_scatter(partial_value.astype(jnp.bfloat16), 'narrow', scatter_di...  131 us
    reduce_scatter x2, waiting for transfers between devices, branch_total(): lax.psum_scatter(rounded.astype(jnp.bfloat16), 'narrow', scatter_dimensio...  117 us
    psum x4, blocking collectives, feature_totals(): return lax.psum((left_sum, right_sum), 'narrow')  73.8 us
    reduce_scatter x1, waiting for transfers between devices, per_device(): lax.psum_scatter(grad_ada_part, 'wide', scatter_dimension=0, tiled=True)  66.1 us
    reduce_scatter x1, waiting for transfers between devices, per_device(): lax.psum_scatter(grad_fc1_part, 'wide', scatter_dimension=0, tiled=True)  55.5 us
    reduce_scatter x1, waiting for transfers between devices, per_device(): lax.psum_scatter(grad_qkv_part, 'wide', scatter_dimension=0, tiled=True)  50.1 us
  transfers between devices with their start and end apart: 19, of which 16 were waited for; matrix products, arithmetic and copies ran while one was open for 9% of the time, Pallas kernels for 0%

commit v1 on v0

v1 whole, which is shorter than its diff:
```python
import jax
import jax.numpy as jnp
from jax import lax
from jax.sharding import Mesh
from jax.sharding import PartitionSpec as P

HEADS = 16


norm_epsilon = 1e-06
gelu_factor = 0.7978845608028654
gelu_cubic = 0.044715


def gelu_tanh(values):
    return (
        0.5
        * values
        * (1.0 + jnp.tanh(gelu_factor * (values + gelu_cubic * values * values * values)))
    )


def gelu_slope(values):
    inner = jnp.tanh(gelu_factor * (values + gelu_cubic * values * values * values))
    return 0.5 * (1.0 + inner) + 0.5 * values * (1.0 - inner * inner) * gelu_factor * (
        1.0 + 3.0 * gelu_cubic * values * values
    )


def norm_forward(values):
    row_mean = jnp.mean(values, axis=1, keepdims=True)
    row_var = jnp.mean(values * values, axis=1, keepdims=True) - row_mean * row_mean
    inverse = lax.rsqrt(row_var + norm_epsilon)
    return (values - row_mean) * inverse, inverse


def norm_backward(grad_normed, normed, inverse):
    mean_one = jnp.mean(grad_normed, axis=1, keepdims=True)
    mean_two = jnp.mean(grad_normed * normed, axis=1, keepdims=True)
    return inverse * (grad_normed - mean_one - normed * mean_two)


def swap_core(values):
    return lax.ppermute(values, "core", [(0, 1), (1, 0)])


def pair_gather(rows):
    other = swap_core(rows)
    mine_first = lax.axis_index("core") == 0
    return jnp.concatenate(
        [jnp.where(mine_first, rows, other), jnp.where(mine_first, other, rows)], axis=0
    )


def pair_scatter(partial):
    half = partial.shape[0] // 2
    core = lax.axis_index("core")
    sent = lax.dynamic_slice_in_dim(partial, (1 - core) * half, half, 0)
    kept = lax.dynamic_slice_in_dim(partial, core * half, half, 0)
    return kept.astype(jnp.float32) + swap_core(sent).astype(jnp.float32)


def shift_narrow(values, step):
    size = lax.axis_size("narrow")
    return lax.ppermute(values, "narrow", [(i, (i + step) % size) for i in range(size)])


def flip_col(values, bit):
    size = lax.axis_size("col")
    return lax.ppermute(values, "col", [(i, i ^ bit) for i in range(size)])


def col_bits():
    bits = []
    bit = 1
    while bit < lax.axis_size("col"):
        bits.append(bit)
        bit *= 2
    return bits


def gather_chips(shard):
    half = shard.shape[0] // 2
    up = shift_narrow(shard, 1)
    down = shift_narrow(shard, -1)
    far = jnp.concatenate([shift_narrow(up[:half], 1), shift_narrow(down[half:], -1)], axis=0)
    line = jnp.stack([shard, up, far, down])
    bits = col_bits()
    sides = []
    for part, order in ((line[:, :half], bits), (line[:, half:], bits[::-1])):
        pieces = {0: part}
        for bit in order:
            for mask in list(pieces):
                pieces[mask | bit] = flip_col(pieces[mask], bit)
        sides.append(jnp.stack([pieces[mask] for mask in range(len(pieces))]))
    return sides


def arrange(sides, low, high):
    col = lax.axis_index("col")
    count = lax.axis_size("col")
    blocks = []
    for side in sides:
        cut = side[..., low:high]
        blocks.append(
            jnp.stack(
                [lax.dynamic_index_in_dim(cut, c ^ col, 0, keepdims=False) for c in range(count)],
                axis=1,
            )
        )
    return jnp.concatenate(blocks, axis=2)


def add_low(left, right):
    return (left.astype(jnp.float32) + right.astype(jnp.float32)).astype(jnp.bfloat16)


def scatter_chips(blocks):
    col = lax.axis_index("col")
    count = lax.axis_size("col")
    half = blocks.shape[2] // 2
    bits = col_bits()
    halves = []
    for part, order in ((blocks[:, :, :half], bits), (blocks[:, :, half:], bits[::-1])):
        pieces = {
            mask: lax.dynamic_index_in_dim(part, mask ^ col, 1, keepdims=False)
            for mask in range(count)
        }
        for bit in order:
            for mask in [m for m in pieces if not m & bit]:
                pieces[mask] = add_low(pieces[mask], flip_col(pieces.pop(mask | bit), bit))
        halves.append(pieces[0])
    line = jnp.concatenate(halves, axis=1)
    own, up, far, down = line[0], line[1], line[2], line[3]
    up_low = add_low(up[:half], shift_narrow(far[:half], -1))
    down_high = add_low(down[half:], shift_narrow(far[half:], 1))
    up_all = jnp.concatenate([up_low, up[half:]], axis=0)
    down_all = jnp.concatenate([down[:half], down_high], axis=0)
    return (
        own.astype(jnp.float32)
        + shift_narrow(up_all, -1).astype(jnp.float32)
        + shift_narrow(down_all, 1).astype(jnp.float32)
    )


def core_rows(values, split_axis, concat_axis):
    return lax.all_to_all(values, "core", split_axis, concat_axis, tiled=True)


def to_images(values, seq_count, half):
    width = values.shape[1]
    shaped = core_rows(values.reshape(seq_count, 2, half, width), 1, 0)
    return lax.all_to_all(
        shaped.reshape(2 * seq_count, half, width), "narrow", 0, 2, tiled=True
    ).reshape(half, -1)


def from_images(values, seq_count):
    half = values.shape[0]
    shaped = lax.all_to_all(values[None], "narrow", 2, 0, tiled=True)
    return core_rows(shaped[:, None], 0, 1).reshape(seq_count * 2 * half, -1)


def per_device(
    tokens,
    condition,
    w_ada,
    b_ada,
    w_qkv,
    b_qv,
    w_proj,
    b_proj,
    w_fc1,
    b_fc1,
    w_fc2,
    b_fc2,
    cotangent,
):
    seq_count = condition.shape[0]
    length = tokens.shape[0] // seq_count
    half = length // 2
    feature_count = condition.shape[1]
    head_dim = feature_count // HEADS
    score_scale = head_dim ** (-0.5)
    narrow = lax.axis_index("narrow")
    col = lax.axis_index("col")
    core = lax.axis_index("core")
    n_size = lax.axis_size("narrow")
    w_size = 2 * lax.axis_size("col")
    wide = 2 * col + core
    part_width = feature_count // 2
    head_count = part_width // head_dim
    unit = feature_count // n_size
    pair = unit // 2
    fc_unit = w_fc1.shape[1]
    fc_half = fc_unit // 2
    rows_low = w_fc1.shape[0]
    rows = 2 * rows_low

    def attend(seq_block):
        outputs = []
        lse_list = []
        for head_index in range(head_count):
            offset = head_index * head_dim
            query_rows = seq_block[0][:, offset : offset + head_dim]
            key_rows = seq_block[1][:, offset : offset + head_dim]
            value_rows = seq_block[2][:, offset : offset + head_dim]
            scores = (
                jnp.einsum("qd,kd->qk", query_rows, key_rows, preferred_element_type=jnp.float32)
                * score_scale
            )
            row_top = jnp.max(scores, axis=1, keepdims=True)
            raised = jnp.exp(scores - row_top)
            row_total = jnp.sum(raised, axis=1, keepdims=True)
            soft_weights = (raised / row_total).astype(jnp.bfloat16)
            outputs.append(jnp.dot(soft_weights, value_rows, preferred_element_type=jnp.float32))
            lse_list.append(row_top[:, 0] + jnp.log(row_total[:, 0]))
        return (jnp.concatenate(outputs, axis=1), jnp.stack(lse_list))

    def attend_back(packed):
        seq_block, lse_rows, grad_block = packed
        pieces = []
        for head_index in range(head_count):
            offset = head_index * head_dim
            query_rows = seq_block[0][:, offset : offset + head_dim]
            key_rows = seq_block[1][:, offset : offset + head_dim]
            value_rows = seq_block[2][:, offset : offset + head_dim]
            grad_head = grad_block[:, offset : offset + head_dim]
            scores = (
                jnp.einsum("qd,kd->qk", query_rows, key_rows, preferred_element_type=jnp.float32)
                * score_scale
            )
            soft_float = jnp.exp(scores - lse_rows[head_index][:, None])
            soft_weights = soft_float.astype(jnp.bfloat16)
            grad_value = jnp.einsum(
                "qk,qd->kd", soft_weights, grad_head, preferred_element_type=jnp.float32
            )
            grad_soft = jnp.einsum(
                "qd,kd->qk", grad_head, value_rows, preferred_element_type=jnp.float32
            )
            inner = jnp.sum(soft_float * grad_soft, axis=1, keepdims=True)
            grad_scores = (soft_float * (grad_soft - inner)).astype(jnp.bfloat16)
            grad_query = (
                jnp.dot(grad_scores, key_rows, preferred_element_type=jnp.float32) * score_scale
            )
            grad_key = (
                jnp.einsum("qk,qd->kd", grad_scores, query_rows, preferred_element_type=jnp.float32)
                * score_scale
            )
            pieces.append([grad_query, grad_key, grad_value])
        return jnp.concatenate(
            [piece[c] for c in range(3) for piece in pieces], axis=1
        ).astype(jnp.bfloat16)


    def turned(values, axis):
        return jnp.take(values, (narrow - jnp.arange(n_size)) % n_size, axis=axis)

    qkv_cut = core_rows(jnp.transpose(w_qkv, (1, 0, 2)), 2, 1)
    proj_cut = core_rows(w_proj, 0, 1).T
    fc1_cut = core_rows(w_fc1, 1, 0)
    fc2_cut = core_rows(w_fc2, 0, 1).T
    pack_one = jnp.concatenate([qkv_cut[0], qkv_cut[1], qkv_cut[2], proj_cut], axis=1)
    sides_one = gather_chips(pack_one)
    pack_two = jnp.concatenate([fc1_cut, fc2_cut], axis=1)
    sides_two = gather_chips(pack_two)

    def matrix(sides, low, high):
        blocks = arrange(sides, low, high)
        return jnp.transpose(blocks, (1, 2, 0, 3)).reshape(feature_count, -1)

    qkv_mats = [matrix(sides_one, c * pair, (c + 1) * pair) for c in range(3)]
    qkv_full = jnp.concatenate(qkv_mats, axis=1)
    proj_full = matrix(sides_one, 3 * pair, 4 * pair)
    fc1_full = matrix(sides_two, 0, fc_half)
    fc2_full = matrix(sides_two, fc_half, 2 * fc_half)

    inputs = to_images(tokens, seq_count, half).astype(jnp.float32)
    small = jnp.concatenate(
        [
            b_ada.reshape(-1),
            b_qv.reshape(-1),
            b_proj,
            b_fc2,
            b_fc1,
            condition.reshape(-1),
        ]
    )
    smalls = lax.all_gather(small, ("narrow", "col", "core"))
    part = b_proj.shape[0]

    def full_bias(low, count):
        return jnp.transpose(
            smalls[:, low : low + count * part].reshape(n_size * w_size, count, part), (1, 0, 2)
        ).reshape(count, feature_count)

    ada_bias = full_bias(0, 6).astype(jnp.float32)
    qv_bias = full_bias(6 * part, 2)
    proj_bias = full_bias(8 * part, 1).astype(jnp.float32)
    fc2_bias = full_bias(9 * part, 1).astype(jnp.float32)
    fc1_size = b_fc1.shape[0]
    fc1_rows = smalls[:, 10 * part : 10 * part + fc1_size].reshape(n_size, 2, fc_half)
    fc1_bias = turned(lax.dynamic_index_in_dim(fc1_rows, core, 1, keepdims=False), 0)
    fc1_bias = fc1_bias.reshape(1, -1).astype(jnp.float32)
    qv_rows = lax.dynamic_index_in_dim(
        qv_bias.reshape(2, n_size, 2, pair), core, 2, keepdims=False
    )
    qv_rows = turned(qv_rows, 1).reshape(2, -1).astype(jnp.float32)
    qkv_bias = jnp.concatenate([qv_rows[0], jnp.zeros_like(qv_rows[0]), qv_rows[1]])

    cond_all = smalls[:w_size, 10 * part + fc1_size :].reshape(-1, feature_count)
    cond_act_all = jax.nn.silu(cond_all.astype(jnp.float32)).astype(jnp.bfloat16)
    cond_cols = lax.dynamic_slice_in_dim(cond_act_all, wide * rows_low, rows_low, 1)
    mod_part = jnp.einsum("sd,dcn->scn", cond_cols, w_ada, preferred_element_type=jnp.float32)
    mod_total = lax.psum(mod_part, ("col", "core"))
    mod_rows = lax.dynamic_slice_in_dim(mod_total, col * n_size, n_size, 0)
    modulation = lax.all_to_all(mod_rows, "narrow", 0, 2, tiled=True).reshape(6, -1) + ada_bias
    shift_one, scale_one, gate_one, shift_two, scale_two, gate_two = [
        modulation[i : i + 1] for i in range(6)
    ]

    normed_one, inverse_one = norm_forward(inputs)
    hidden_one = (normed_one * (1.0 + scale_one) + shift_one).astype(jnp.bfloat16)
    hidden_one_full = pair_gather(hidden_one)
    qkv_low = (
        jnp.dot(hidden_one_full, qkv_full, preferred_element_type=jnp.float32) + qkv_bias
    ).astype(jnp.bfloat16)
    qkv_parts = [qkv_low[:, c * part_width : (c + 1) * part_width] for c in range(3)]
    attended, lse_rows = attend(qkv_parts)
    attended_low = attended.astype(jnp.bfloat16)
    attn_branch = (
        pair_scatter(
            jnp.einsum(
                "th,dh->td", attended_low, proj_full, preferred_element_type=jnp.float32
            ).astype(jnp.bfloat16)
        )
        + proj_bias
    )
    residual = inputs + attn_branch * gate_one
    normed_two, inverse_two = norm_forward(residual)
    hidden_two = (normed_two * (1.0 + scale_two) + shift_two).astype(jnp.bfloat16)
    hidden_two_full = pair_gather(hidden_two)
    grad_out = to_images(cotangent, seq_count, half).astype(jnp.float32)
    grad_mlp = (grad_out * gate_two).astype(jnp.bfloat16)
    grad_mlp_full = pair_gather(grad_mlp)
    pre_act = jnp.dot(hidden_two_full, fc1_full, preferred_element_type=jnp.float32) + fc1_bias
    activated = gelu_tanh(pre_act).astype(jnp.bfloat16)
    grad_act = jnp.dot(grad_mlp_full, fc2_full, preferred_element_type=jnp.float32)
    grad_pre = (grad_act * gelu_slope(pre_act)).astype(jnp.bfloat16)

    def blocked(grad):
        return jnp.transpose(
            grad.astype(jnp.bfloat16).reshape(-1, rows, n_size, grad.shape[1] // n_size),
            (2, 0, 1, 3),
        )

    grad_fc1_part = jnp.einsum(
        "td,tf->df", hidden_two_full, grad_pre, preferred_element_type=jnp.float32
    )
    grad_fc2_part = jnp.einsum(
        "td,tf->df", grad_mlp_full, activated, preferred_element_type=jnp.float32
    )
    total_fc1 = scatter_chips(blocked(grad_fc1_part))
    total_fc2 = scatter_chips(blocked(grad_fc2_part))
    grad_hidden_two = pair_scatter(
        jnp.einsum("tf,df->td", grad_pre, fc1_full, preferred_element_type=jnp.float32).astype(
            jnp.bfloat16
        )
    )
    mlp_branch = (
        pair_scatter(
            jnp.einsum(
                "tf,df->td", activated, fc2_full, preferred_element_type=jnp.float32
            ).astype(jnp.bfloat16)
        )
        + fc2_bias
    )
    output = from_images((residual + mlp_branch * gate_two).astype(jnp.bfloat16), seq_count)

    grad_residual = grad_out + norm_backward(
        grad_hidden_two * (1.0 + scale_two), normed_two, inverse_two
    )
    grad_attn = (grad_residual * gate_one).astype(jnp.bfloat16)
    grad_attn_full = pair_gather(grad_attn)
    grad_proj_part = jnp.einsum(
        "td,th->dh", grad_attn_full, attended_low, preferred_element_type=jnp.float32
    )
    grad_attended = jnp.dot(
        grad_attn_full, proj_full, preferred_element_type=jnp.float32
    ).astype(jnp.bfloat16)
    grad_qkv = attend_back((qkv_parts, lse_rows, grad_attended))
    grad_hidden_one = pair_scatter(
        jnp.einsum("tn,dn->td", grad_qkv, qkv_full, preferred_element_type=jnp.float32).astype(
            jnp.bfloat16
        )
    )
    grad_qkv_part = jnp.einsum(
        "td,tn->dn", hidden_one_full, grad_qkv, preferred_element_type=jnp.float32
    )
    grad_inputs = grad_residual + norm_backward(
        grad_hidden_one * (1.0 + scale_one), normed_one, inverse_one
    )
    grad_tokens = from_images(grad_inputs.astype(jnp.bfloat16), seq_count).astype(jnp.float32)
    total_one = scatter_chips(
        jnp.concatenate(
            [blocked(grad_qkv_part[:, c * part_width : (c + 1) * part_width]) for c in range(3)]
            + [blocked(grad_proj_part)],
            axis=3,
        )
    )

    def sums(values):
        return jnp.sum(values.astype(jnp.float32), axis=0)

    packed = jnp.concatenate(
        [
            sums(grad_hidden_one),
            sums(grad_hidden_one * normed_one),
            sums(grad_residual * attn_branch),
            sums(grad_hidden_two),
            sums(grad_hidden_two * normed_two),
            sums(grad_out * mlp_branch),
            sums(grad_mlp),
            sums(grad_attn),
            turned(sums(grad_pre).reshape(n_size, fc_half), 0).reshape(-1),
            turned(sums(grad_qkv[:, :part_width]).reshape(n_size, pair), 0).reshape(-1),
            turned(sums(grad_qkv[:, 2 * part_width :]).reshape(n_size, pair), 0).reshape(-1),
        ]
    )
    packs = lax.all_gather(packed, ("col", "narrow", "core"))
    packs = packs.reshape(-1, 2, packed.shape[0])
    d = feature_count
    grad_mod = jnp.sum(packs[:, :, : 6 * d], axis=1).astype(jnp.bfloat16).reshape(-1, 6, d)
    cores = jnp.sum(packs[:, :, 6 * d :], axis=0)
    both = jnp.sum(cores[:, : 2 * d], axis=0)
    place = narrow * w_size + wide
    grad_b_fc2 = lax.dynamic_slice_in_dim(both[:d], place * part, part, 0)
    grad_b_proj = lax.dynamic_slice_in_dim(both[d:], place * part, part, 0)
    fc1_sums = jnp.transpose(
        cores[:, 2 * d : 2 * d + n_size * fc_half].reshape(2, n_size, fc_half), (1, 0, 2)
    ).reshape(-1)
    grad_b_fc1 = lax.dynamic_slice_in_dim(fc1_sums, place * fc1_size, fc1_size, 0)
    qv_sums = jnp.transpose(
        cores[:, 2 * d + n_size * fc_half :].reshape(2, 2, n_size, pair), (1, 2, 0, 3)
    ).reshape(2, d)
    grad_b_qv = lax.dynamic_slice_in_dim(qv_sums, place * part, part, 1)
    ada_sums = jnp.sum(grad_mod.astype(jnp.float32), axis=0)
    grad_b_ada = lax.dynamic_slice_in_dim(ada_sums, place * part, part, 1)
    mod_slice = lax.dynamic_slice_in_dim(grad_mod, narrow * unit, unit, 2)
    grad_w_ada = jnp.einsum(
        "sd,scn->dcn", cond_cols, mod_slice, preferred_element_type=jnp.float32
    )
    cond_part = jnp.einsum("scn,dcn->sd", mod_slice, w_ada, preferred_element_type=jnp.float32)
    cond_parts = lax.all_gather(cond_part, ("narrow", "col", "core"))
    cond_rows = lax.dynamic_slice_in_dim(cond_parts, wide * seq_count, seq_count, 1)
    cond_sum = jnp.sum(cond_rows.reshape(n_size, w_size, seq_count, rows_low), axis=0)
    cond_total = jnp.transpose(cond_sum, (1, 0, 2)).reshape(seq_count, d)
    cond_float = condition.astype(jnp.float32)
    sigmoid_cond = jax.nn.sigmoid(cond_float)
    grad_cond = cond_total * sigmoid_cond * (1.0 + cond_float * (1.0 - sigmoid_cond))

    low_one = total_one.astype(jnp.bfloat16)
    qkv_out = jnp.stack([low_one[:, c * pair : (c + 1) * pair] for c in range(3)])
    grad_w_qkv = jnp.transpose(core_rows(qkv_out, 1, 2).astype(jnp.float32), (1, 0, 2))
    grad_w_proj = core_rows(low_one[:, 3 * pair :].T, 1, 0).astype(jnp.float32)
    grad_w_fc1 = core_rows(total_fc1.astype(jnp.bfloat16), 0, 1).astype(jnp.float32)
    grad_w_fc2 = core_rows(total_fc2.astype(jnp.bfloat16).T, 1, 0).astype(jnp.float32)
    return (
        output,
        grad_tokens,
        grad_cond,
        grad_w_ada,
        grad_b_ada,
        grad_w_qkv,
        grad_b_qv,
        grad_w_proj,
        grad_b_proj,
        grad_w_fc1,
        grad_b_fc1,
        grad_w_fc2,
        grad_b_fc2,
    )


W = ("col", "core")
NW = ("narrow", "col", "core")


def solution(mesh):
    devices = mesh.devices
    split = Mesh(devices.reshape(devices.shape[0], devices.shape[1] // 2, 2), NW)
    return jax.shard_map(
        per_device,
        mesh=split,
        in_specs=(
            P(W, "narrow"),
            P(W, None),
            P(W, None, "narrow"),
            P(None, NW),
            P(W, None, "narrow"),
            P(None, NW),
            P("narrow", W),
            P(NW),
            P(W, "narrow"),
            P(NW),
            P("narrow", W),
            P(NW),
            P(W, "narrow"),
        ),
        out_specs=(
            P(W, "narrow"),
            P(W, "narrow"),
            P(W, None),
            P(W, None, "narrow"),
            P(None, NW),
            P(W, None, "narrow"),
            P(None, NW),
            P("narrow", W),
            P(NW),
            P(W, "narrow"),
            P(NW),
            P("narrow", W),
            P(NW),
        ),
        check_vma=False,
    )
```

time: 1250 us -> 957 us (0.77)
  waiting for transfers between devices: 845 us -> 305 us
  starting transfers between devices: 1.35 us -> 119 us
  local copies, waits for them, and re-layouts: 35.3 us -> 149 us
  other arithmetic: 49 us -> 140 us
  blocking collectives: 141 us -> 68 us
    reduce_scatter x9 -> x0, waiting for transfers between devices: 495 us -> none  [the longest x2 131 us: feature_grads(): lax.psum_scatter(partial_value.astype(jnp.bfloat16), 'narrow', scatter_di...]
    all_gather x8 -> x1, waiting for transfers between devices: 347 us -> 0.01 us  [per_device(): packs = lax.all_gather(packed, ('col', 'narrow', 'core'))]
    unnamed x21 -> x4, waiting for transfers between devices: 2.86 us -> 119 us
    ppermute x0 -> x58, waiting for transfers between devices: none -> 88.6 us  [the longest x30 67.4 us: flip_col(): return lax.ppermute(values, 'col', [(i, i ^ bit) for i in range(size)])]
    ppermute x0 -> x58, starting transfers between devices: none -> 75.2 us  [the longest x20 37.7 us: shift_narrow(): lax.ppermute(values, 'narrow', [(i, (i + step) % size) for i in range(siz...]
    psum x4 -> x0, blocking collectives: 73.8 us -> none  [feature_totals(): return lax.psum((left_sum, right_sum), 'narrow')]
    all_to_all x0 -> x11, waiting for transfers between devices: none -> 60.3 us  [the longest x2 36.8 us: to_images(): lax.all_to_all(shaped.reshape(2 * seq_count, half, width), 'narrow', 0, 2...]
    all_to_all x0 -> x11, starting transfers between devices: none -> 44 us  [the longest x6 22.5 us: core_rows(): return lax.all_to_all(values, 'core', split_axis, concat_axis, tiled=True)]
  transfers between devices with their start and end apart: 19 -> 72, of which waited for: 16 -> 23; matrix products, arithmetic and copies ran while one was open for 9% -> 38% of each run, Pallas kernels for 0% -> 0%
where the time goes in v1:
time: 957 us; the launch traced here: 945 us
  waiting for transfers between devices  305 us (32%)
  local copies, waits for them, and re-layouts  149 us (16%)
  matrix products  147 us (15%)
  other arithmetic  140 us (15%)
  starting transfers between devices  119 us (12%)
  blocking collectives  68 us (7%)
  between operations  16.4 us (2%)
    unnamed x4, waiting for transfers between devices  119 us
    ppermute x30, waiting for transfers between devices, flip_col(): return lax.ppermute(values, 'col', [(i, i ^ bit) for i in range(size)])  67.4 us
    all_gather x1, blocking collectives, per_device(): cond_parts = lax.all_gather(cond_part, ('narrow', 'col', 'core'))  40.2 us
    ppermute x20, starting transfers between devices, shift_narrow(): lax.ppermute(values, 'narrow', [(i, (i + step) % size) for i in range(siz...  37.7 us
    ppermute x30, starting transfers between devices, flip_col(): return lax.ppermute(values, 'col', [(i, i ^ bit) for i in range(size)])  37 us
    psum x1, waiting for transfers between devices, per_device(): mod_total = lax.psum(mod_part, ('col', 'core'))  36.8 us
    all_to_all x2, waiting for transfers between devices, to_images(): lax.all_to_all(shaped.reshape(2 * seq_count, half, width), 'narrow', 0, 2...  36.8 us
    unnamed x306, local copies, waits for them, and re-layouts  36.1 us
  transfers between devices with their start and end apart: 72, of which 23 were waited for; matrix products, arithmetic and copies ran while one was open for 38% of the time, Pallas kernels for 0%

profile of v1, /device:TPU:0, one launch (start us, length us, event | category | flops | bytes accessed | tf_op | source)
XLA Modules:
  0.0 944.7 jit_solution(18357716593657949926)
XLA Ops:
  7.2 3.4 all-to-all-start.4
  12.4 3.4 all-to-all-start.3
  23.8 3.4 all-to-all-start.6
  28.8 3.4 all-to-all-start.5
  34.8 3.8 collective-permute-start.15
  47.3 119.2 %all-reduce.6.cloned.1.call-done = bf16[79872]{0:T(1024)(128)(2,1)} async-done(((bf16[79872]{0:T(1024)(128)(2,1)}), bf16[79872]{0:T(1024)(128)(2,1)}) %all-reduce.6.cloned.1.call-update) | async-done | bytes 159760
  173.8 4.5 collective-permute-start.2
  189.2 36.8 %all-reduce.4.cloned.1.call-done = f32[16,6,256]{2,0,1:T(8,128)} async-done(((f32[16,6,256]{2,0,1:T(8,128)}), f32[16,6,256]{2,0,1:T(8,128)}) %all-reduce.4.cloned.1.call-update) | async-done | bytes 98320 | tf_op jit(solution)/shard_map/psum | solution.py:315
  227.4 4.6 all-to-all-start.2
  247.5 4.5 all-to-all-start
  261.2 6.8 collective-permute-done.5
  272.9 6.3 collective-permute-done.8
  281.2 9.2 collective-permute-done.10
  298.8 5.4 all_to_all.237
  304.2 3.5 all-to-all-start.1
  316.3 17.7 %all-to-all-done.1 = bf16[4,512,256]{2,1,0:T(8,128)(2,1)S(1)} async-done(((bf16[4,512,256]{2,1,0:T(8,128)(2,1)}), bf16[4,512,256]{2,1,0:T(8,128)(2,1)S(1)}, u32[]{:S(2)}, u32[]{:S(2)}) %all-to-all-start.1) | async-done | bytes 1048608 | tf_op jit(solution)/shard_map/all_to_all | solution.py:153
  334.0 4.8 all-to-all-start.10
  345.2 19.1 %all-to-all-done.10 = bf16[4,512,256]{2,1,0:T(8,128)(2,1)} async-done(((bf16[4,512,256]{2,1,0:T(8,128)(2,1)}), bf16[4,512,256]{2,1,0:T(8,128)(2,1)}, u32[]{:S(2)}, u32[]{:S(2)}) %all-to-all-start.10) | async-done | bytes 1048608 | tf_op jit(solution)/shard_map/all_to_all | solution.py:153
  373.5 7.2 add_convert_fusion
  420.8 3.2 copy.243
  426.3 3.2 copy.245
  431.7 4.5 fusion.55
  436.3 6.6 convolution_convert_fusion.5
  442.9 12.1 %convert_reduce_fusion = (f32[2048]{0:T(1024)S(1)}, bf16[1024,2048]{1,0:T(8,128)(2,1)}) fusion(f32[1024,2048]{1,0:T(8,128)S(1)} %fusion.55, f32[2048]{0:T(1024)S(1)} %bitcast.605, bf16[1024,2048]{1,0:T(8,128)(2,1)S(1)} %bitcast.533, bf16[512,1024]{1,0:T(8,128)(2,1)S(1)} %copy-done.82, bf16[512,1024]{1,0:T(8,128)(2,1)S(1)} %get-tuple-element.64), kind=kOutput, calls=%fused_computation.14 | convolution fusion | flops 4345296896 | bytes 18890752 | tf_op jit(solution)/shard_map/dot_general | solution.py:348
  455.0 6.7 convolution_convert_fusion.1
  461.7 5.9 convolution_convert_fusion.4
  467.6 6.1 convolution_convert_fusion.2
  475.1 7.8 reshape.584
  493.8 8.0 reshape.581
  507.6 7.3 collective-permute-done.49
  520.3 5.4 collective-permute-done.39
  525.8 3.9 collective-permute-done.42
  532.0 7.5 collective-permute-done.50
  547.5 8.3 collective-permute-done.38
  558.4 4.9 collective-permute-done.41
  563.3 3.9 collective-permute-start.44
  569.9 3.7 multiply_reduce_fusion.16
  573.6 4.6 copy.246
  578.8 8.0 reduce.13
  586.8 3.8 reshape.685
  590.6 5.1 all-to-all-start.7
  635.7 4.6 multiply_convert_fusion.8
  642.9 3.3 multiply_convert_fusion.1
  646.2 4.6 multiply_convert_fusion.2
  650.8 4.6 multiply_convert_fusion.3
  655.5 4.7 multiply_convert_fusion.4
  660.1 4.6 multiply_convert_fusion.5
  664.8 4.7 multiply_convert_fusion.6
  669.4 4.6 multiply_convert_fusion.7
  713.6 6.9 convolution_convert_fusion.3
  720.5 5.0 convolution_convert_fusion
  747.7 5.6 collective-permute-done.29
  782.2 14.6 %collective-permute-done.36 = bf16[128,512]{1,0:T(8,128)(2,1)S(1)} collective-permute-done((bf16[128,512]{1,0:T(8,128)(2,1)S(1)}, bf16[128,512]{1,0:T(8,128)(2,1)S(1)}, u32[]{:S(2)}, u32[]{:S(2)}) %collective-permute-start.36) | collective-permute-done | bytes 131104 | tf_op jit(solution)/shard_map/ppermute | solution.py:65
  802.8 4.3 collective-permute-start.35
  809.8 4.3 all-to-all-start.16
  822.1 7.0 reduce.14
  832.6 4.7 all_to_all.238
  837.3 4.6 all_to_all.239
  841.9 4.6 all_to_all.240
  846.4 3.9 all_to_all.241
  850.4 3.5 all-to-all-start.11
  860.0 20.1 %all-to-all-done.11 = bf16[4,2,65536]{2,1,0:T(2,128)(2,1)S(1)} async-done(((bf16[4,2,65536]{2,1,0:T(2,128)(2,1)}), bf16[4,2,65536]{2,1,0:T(2,128)(2,1)S(1)}, u32[]{:S(2)}, u32[]{:S(2)}) %all-to-all-start.11) | async-done | bytes 1048608 | tf_op jit(solution)/shard_map/all_to_all | solution.py:160
  882.0 4.8 all_to_all.242
  896.5 40.2 %all-gather.2 = f32[512,128]{1,0:T(8,128)S(1)} all-gather(f32[16,128]{1,0:T(8,128)S(1)} %convolution_bitcast_fusion), channel_id=4, replica_groups=mesh['narrow'=4,'col'=4,'core'=2] {'narrow','col','core'}, dimensions={0}, use_global_device_ids=true | all-gather | bytes 270336 | tf_op jit(solution)/shard_map/all_gather | solution.py:454
  (707 shorter events, 360.7 us)
Async XLA Ops:
  18.7 154.2 %collective-permute-start.1 = (bf16[256,512]{1,0:T(8,128)(2,1)}, bf16[256,512]{1,0:T(8,128)(2,1)}, u32[]{:S(2)}, u32[]{:S(2)}) collective-permute-start(bf16[256,512]{1,0:T(8,128)(2,1)} %get-tuple-element.153), channel_id=1, source_target_pairs={{0,8},{8,16},{16,24},{24,0},{1,9},{9,17},{17,25},{25,1},{2,10},{10... | collective-permute-start | bytes 786440 | tf_op jit(solution)/shard_map/ppermute | solution.py:65
  21.8 156.6 %collective-permute-start.3 = (bf16[256,512]{1,0:T(8,128)(2,1)}, bf16[256,512]{1,0:T(8,128)(2,1)}, u32[]{:S(2)}, u32[]{:S(2)}) collective-permute-start(bf16[256,512]{1,0:T(8,128)(2,1)} %get-tuple-element.153), channel_id=1, source_target_pairs={{0,24},{8,0},{16,8},{24,16},{1,25},{9,1},{17,9},{25,17},{2,26},{10... | collective-permute-start | bytes 786440 | tf_op jit(solution)/shard_map/ppermute | solution.py:65
  32.2 134.2 %all-reduce.6.cloned.1.call-start = ((), (), s32[]{:S(2)}) async-start(), calls=%async_computation.19 | async-start | bytes 319488
  34.8 197.2 %collective-permute-start.13 = (bf16[256,1024]{1,0:T(8,128)(2,1)}, bf16[256,1024]{1,0:T(8,128)(2,1)S(1)}, u32[]{:S(2)}, u32[]{:S(2)}) collective-permute-start(bf16[256,1024]{1,0:T(8,128)(2,1)} %get-tuple-element.115), channel_id=1, source_target_pairs={{0,8},{8,16},{16,24},{24,0},{1,9},{9,17},{17,25},{25,1},{2,10},{10... | collective-permute-start | bytes 1572872 | tf_op jit(solution)/shard_map/ppermute | solution.py:65
  34.8 199.9 %collective-permute-start.15 = (bf16[256,1024]{1,0:T(8,128)(2,1)}, bf16[256,1024]{1,0:T(8,128)(2,1)}, u32[]{:S(2)}, u32[]{:S(2)}) collective-permute-start(bf16[256,1024]{1,0:T(8,128)(2,1)} %get-tuple-element.115), channel_id=1, source_target_pairs={{0,24},{8,0},{16,8},{24,16},{1,25},{9,1},{17,9},{25,17},{2,26},{10... | collective-permute-start | bytes 1572872 | tf_op jit(solution)/shard_map/ppermute | solution.py:65
  44.3 181.7 %all-reduce.4.cloned.1.call-start = ((), (), s32[]{:S(2)}) async-start(), calls=%async_computation.17 | async-start | bytes 196608 | tf_op jit(solution)/shard_map/psum | solution.py:315
  187.1 71.2 %collective-permute-start.9 = (bf16[4,128,512]{2,1,0:T(8,128)(2,1)}, bf16[4,128,512]{2,1,0:T(8,128)(2,1)}, u32[]{:S(2)}, u32[]{:S(2)}) collective-permute-start(bf16[4,128,512]{2,1,0:T(8,128)(2,1)} %get-tuple-element.100), channel_id=1, source_target_pairs={{0,4},{2,6},{4,0},{6,2},{1,5},{3,7},{5,1},{7,3},{8,12},{10,14},{12... | collective-permute-start | bytes 1572872 | tf_op jit(solution)/shard_map/ppermute | solution.py:70
  227.4 20.1 %all-to-all-start.2 = ((f32[4,6,256]{2,1,0:T(8,128)}), f32[4,6,256]{2,1,0:T(8,128)}, u32[]{:S(2)}, u32[]{:S(2)}) async-start(f32[4,6,256]{2,1,0:T(8,128)} %copy.226), calls=%async_computation.2 | async-start | bytes 65536 | tf_op jit(solution)/shard_map/all_to_all | solution.py:317
  232.7 23.4 %collective-permute-start.14 = (bf16[128,1024]{1,0:T(8,128)(2,1)}, bf16[128,1024]{1,0:T(8,128)(2,1)}, u32[]{:S(2)}, u32[]{:S(2)}) collective-permute-start(bf16[128,1024]{1,0:T(8,128)(2,1)} %slice.660), channel_id=1, source_target_pairs={{0,8},{8,16},{16,24},{24,0},{1,9},{9,17},{17,25},{25,1},{2,10},{10... | collective-permute-start | bytes 786440 | tf_op jit(solution)/shard_map/ppermute | solution.py:65
  236.4 22.4 %collective-permute-start.16 = (bf16[128,1024]{1,0:T(8,128)(2,1)}, bf16[128,1024]{1,0:T(8,128)(2,1)}, u32[]{:S(2)}, u32[]{:S(2)}) collective-permute-start(bf16[128,1024]{1,0:T(8,128)(2,1)} %slice.661), channel_id=1, source_target_pairs={{0,24},{8,0},{16,8},{24,16},{1,25},{9,1},{17,9},{25,17},{2,26},{10... | collective-permute-start | bytes 786440 | tf_op jit(solution)/shard_map/ppermute | solution.py:65
  247.5 51.3 %all-to-all-start = ((bf16[2,2,512,256]{3,2,0,1:T(8,128)(2,1)}), bf16[2,2,512,256]{3,2,0,1:T(8,128)(2,1)}, u32[]{:S(2)}, u32[]{:S(2)}) async-start(bf16[2,2,512,256]{3,2,0,1:T(8,128)(2,1)} %copy.224), calls=%async_computation | async-start | bytes 2097152 | tf_op jit(solution)/shard_map/all_to_all | solution.py:147
  252.8 15.3 %collective-permute-start.5 = (bf16[4,128,512]{2,1,0:T(8,128)(2,1)}, bf16[4,128,512]{2,1,0:T(8,128)(2,1)}, u32[]{:S(2)}, u32[]{:S(2)}) collective-permute-start(bf16[4,128,512]{2,1,0:T(8,128)(2,1)} %get-tuple-element.101), channel_id=1, source_target_pairs={{0,2},{2,0},{4,6},{6,4},{1,3},{3,1},{5,7},{7,5},{8,10},{10,8},{12,... | collective-permute-start | bytes 1572872 | tf_op jit(solution)/shard_map/ppermute | solution.py:70
  256.2 23.0 %collective-permute-start.8 = (bf16[4,128,512]{2,1,0:T(8,128)(2,1)}, bf16[4,128,512]{2,1,0:T(8,128)(2,1)S(1)}, u32[]{:S(2)}, u32[]{:S(2)}) collective-permute-start(bf16[4,128,512]{2,1,0:T(8,128)(2,1)} %get-tuple-element.100), channel_id=1, source_target_pairs={{0,2},{2,0},{4,6},{6,4},{1,3},{3,1},{5,7},{7,5},{8,10},{10,8},{12,... | collective-permute-start | bytes 1572872 | tf_op jit(solution)/shard_map/ppermute | solution.py:70
  256.2 39.0 %collective-permute-start.6 = (bf16[4,128,512]{2,1,0:T(8,128)(2,1)}, bf16[4,128,512]{2,1,0:T(8,128)(2,1)S(1)}, u32[]{:S(2)}, u32[]{:S(2)}) collective-permute-start(bf16[4,128,512]{2,1,0:T(8,128)(2,1)} %get-tuple-element.101), channel_id=1, source_target_pairs={{0,4},{2,6},{4,0},{6,2},{1,5},{3,7},{5,1},{7,3},{8,12},{10,14},{12... | collective-permute-start | bytes 1572872 | tf_op jit(solution)/shard_map/ppermute | solution.py:70
  258.3 32.1 %collective-permute-start.10 = (bf16[4,128,512]{2,1,0:T(8,128)(2,1)}, bf16[4,128,512]{2,1,0:T(8,128)(2,1)S(1)}, u32[]{:S(2)}, u32[]{:S(2)}) collective-permute-start(bf16[4,128,512]{2,1,0:T(8,128)(2,1)} %collective-permute-done.9), channel_id=1, source_target_pairs={{0,2},{2,0},{4,6},{6,4},{1,3},{3,1},{5,7},{7,5},{8,10},{10,8},{12,... | collective-permute-start | bytes 1572872 | tf_op jit(solution)/shard_map/ppermute | solution.py:70
  268.0 27.8 %collective-permute-start.7 = (bf16[4,128,512]{2,1,0:T(8,128)(2,1)}, bf16[4,128,512]{2,1,0:T(8,128)(2,1)S(1)}, u32[]{:S(2)}, u32[]{:S(2)}) collective-permute-start(bf16[4,128,512]{2,1,0:T(8,128)(2,1)} %collective-permute-done.5), channel_id=1, source_target_pairs={{0,4},{2,6},{4,0},{6,2},{1,5},{3,7},{5,1},{7,3},{8,12},{10,14},{12... | collective-permute-start | bytes 1572872 | tf_op jit(solution)/shard_map/ppermute | solution.py:70
  272.3 140.3 %collective-permute-start.20 = (bf16[4,128,1024]{2,1,0:T(8,128)(2,1)}, bf16[4,128,1024]{2,1,0:T(8,128)(2,1)}, u32[]{:S(2)}, u32[]{:S(2)}) collective-permute-start(bf16[4,128,1024]{2,1,0:T(8,128)(2,1)} %get-tuple-element.82), channel_id=1, source_target_pairs={{0,2},{2,0},{4,6},{6,4},{1,3},{3,1},{5,7},{7,5},{8,10},{10,8},{12,... | collective-permute-start | bytes 3145736 | tf_op jit(solution)/shard_map/ppermute | solution.py:70
  279.2 90.7 %collective-permute-start.21 = (bf16[4,128,1024]{2,1,0:T(8,128)(2,1)}, bf16[4,128,1024]{2,1,0:T(8,128)(2,1)}, u32[]{:S(2)}, u32[]{:S(2)}) collective-permute-start(bf16[4,128,1024]{2,1,0:T(8,128)(2,1)} %get-tuple-element.82), channel_id=1, source_target_pairs={{0,4},{2,6},{4,0},{6,2},{1,5},{3,7},{5,1},{7,3},{8,12},{10,14},{12... | collective-permute-start | bytes 3145736 | tf_op jit(solution)/shard_map/ppermute | solution.py:70
  290.4 79.6 %collective-permute-start.17 = (bf16[4,128,1024]{2,1,0:T(8,128)(2,1)}, bf16[4,128,1024]{2,1,0:T(8,128)(2,1)}, u32[]{:S(2)}, u32[]{:S(2)}) collective-permute-start(bf16[4,128,1024]{2,1,0:T(8,128)(2,1)} %get-tuple-element.83), channel_id=1, source_target_pairs={{0,2},{2,0},{4,6},{6,4},{1,3},{3,1},{5,7},{7,5},{8,10},{10,8},{12,... | collective-permute-start | bytes 3145736 | tf_op jit(solution)/shard_map/ppermute | solution.py:70
  295.2 119.6 %collective-permute-start.18 = (bf16[4,128,1024]{2,1,0:T(8,128)(2,1)}, bf16[4,128,1024]{2,1,0:T(8,128)(2,1)}, u32[]{:S(2)}, u32[]{:S(2)}) collective-permute-start(bf16[4,128,1024]{2,1,0:T(8,128)(2,1)} %get-tuple-element.83), channel_id=1, source_target_pairs={{0,4},{2,6},{4,0},{6,2},{1,5},{3,7},{5,1},{7,3},{8,12},{10,14},{12... | collective-permute-start | bytes 3145736 | tf_op jit(solution)/shard_map/ppermute | solution.py:70
  304.2 29.8 %all-to-all-start.1 = ((bf16[4,512,256]{2,1,0:T(8,128)(2,1)}), bf16[4,512,256]{2,1,0:T(8,128)(2,1)S(1)}, u32[]{:S(2)}, u32[]{:S(2)}) async-start(bf16[4,512,256]{2,1,0:T(8,128)(2,1)} %bitcast.3), calls=%async_computation.1 | async-start | bytes 2097152 | tf_op jit(solution)/shard_map/all_to_all | solution.py:153
  334.0 30.3 %all-to-all-start.10 = ((bf16[4,512,256]{2,1,0:T(8,128)(2,1)}), bf16[4,512,256]{2,1,0:T(8,128)(2,1)}, u32[]{:S(2)}, u32[]{:S(2)}) async-start(bf16[4,512,256]{2,1,0:T(8,128)(2,1)} %bitcast.130), calls=%async_computation.10 | async-start | bytes 2097152 | tf_op jit(solution)/shard_map/all_to_all | solution.py:153
  344.0 27.6 %collective-permute-start = (bf16[512,1024]{1,0:T(8,128)(2,1)}, bf16[512,1024]{1,0:T(8,128)(2,1)}, u32[]{:S(2)}, u32[]{:S(2)}) collective-permute-start(bf16[512,1024]{1,0:T(8,128)(2,1)} %add_convert_fusion.4), channel_id=1, source_target_pairs={{0,1},{1,0},{2,3},{3,2},{4,5},{5,4},{6,7},{7,6},{8,9},{9,8},{10,11... | collective-permute-start | bytes 3145736 | tf_op jit(solution)/shard_map/ppermute | solution.py:44
  369.9 39.9 %collective-permute-start.24 = (bf16[512,1024]{1,0:T(8,128)(2,1)S(1)}, bf16[512,1024]{1,0:T(8,128)(2,1)}, u32[]{:S(2)}, u32[]{:S(2)}) collective-permute-start(bf16[512,1024]{1,0:T(8,128)(2,1)S(1)} %multiply_convert_fusion.10), channel_id=1, source_target_pairs={{0,1},{1,0},{2,3},{3,2},{4,5},{5,4},{6,7},{7,6},{8,9},{9,8},{10,11... | collective-permute-start | bytes 3145736 | tf_op jit(solution)/shard_map/ppermute | solution.py:44
  370.0 42.6 %collective-permute-start.22 = (bf16[4,128,1024]{2,1,0:T(8,128)(2,1)}, bf16[4,128,1024]{2,1,0:T(8,128)(2,1)}, u32[]{:S(2)}, u32[]{:S(2)}) collective-permute-start(bf16[4,128,1024]{2,1,0:T(8,128)(2,1)} %collective-permute-done.21), channel_id=1, source_target_pairs={{0,2},{2,0},{4,6},{6,4},{1,3},{3,1},{5,7},{7,5},{8,10},{10,8},{12,... | collective-permute-start | bytes 3145736 | tf_op jit(solution)/shard_map/ppermute | solution.py:70
  371.5 43.3 %collective-permute-start.19 = (bf16[4,128,1024]{2,1,0:T(8,128)(2,1)}, bf16[4,128,1024]{2,1,0:T(8,128)(2,1)}, u32[]{:S(2)}, u32[]{:S(2)}) collective-permute-start(bf16[4,128,1024]{2,1,0:T(8,128)(2,1)} %collective-permute-done.17), channel_id=1, source_target_pairs={{0,4},{2,6},{4,0},{6,2},{1,5},{3,7},{5,1},{7,3},{8,12},{10,14},{12... | collective-permute-start | bytes 3145736 | tf_op jit(solution)/shard_map/ppermute | solution.py:70
  420.0 10.9 %collective-permute-start.12 = (bf16[512,1024]{1,0:T(8,128)(2,1)S(1)}, bf16[512,1024]{1,0:T(8,128)(2,1)S(1)}, u32[]{:S(2)}, u32[]{:S(2)}) collective-permute-start(bf16[512,1024]{1,0:T(8,128)(2,1)S(1)} %add_convert_fusion.3), channel_id=1, source_target_pairs={{0,1},{1,0},{2,3},{3,2},{4,5},{5,4},{6,7},{7,6},{8,9},{9,8},{10,11... | collective-permute-start | bytes 3145736 | tf_op jit(solution)/shard_map/ppermute | solution.py:44
  488.6 43.2 %collective-permute-start.48 = (bf16[4,128,512]{2,1,0:T(8,128)(2,1)}, bf16[4,128,512]{2,1,0:T(8,128)(2,1)S(1)}, u32[]{:S(2)}, u32[]{:S(2)}) collective-permute-start(bf16[4,128,512]{2,1,0:T(8,128)(2,1)} %get-tuple-element.48), channel_id=1, source_target_pairs={{0,2},{2,0},{4,6},{6,4},{1,3},{3,1},{5,7},{7,5},{8,10},{10,8},{12,... | collective-permute-start | bytes 1572872 | tf_op jit(solution)/shard_map/ppermute | solution.py:70
  490.6 24.3 %collective-permute-start.49 = (bf16[4,128,512]{2,1,0:T(8,128)(2,1)}, bf16[4,128,512]{2,1,0:T(8,128)(2,1)}, u32[]{:S(2)}, u32[]{:S(2)}) collective-permute-start(bf16[4,128,512]{2,1,0:T(8,128)(2,1)} %get-tuple-element.49), channel_id=1, source_target_pairs={{0,2},{2,0},{4,6},{6,4},{1,3},{3,1},{5,7},{7,5},{8,10},{10,8},{12,... | collective-permute-start | bytes 1572872 | tf_op jit(solution)/shard_map/ppermute | solution.py:70
  491.7 50.6 %collective-permute-start.51 = (bf16[4,128,512]{2,1,0:T(8,128)(2,1)}, bf16[4,128,512]{2,1,0:T(8,128)(2,1)S(1)}, u32[]{:S(2)}, u32[]{:S(2)}) collective-permute-start(bf16[4,128,512]{2,1,0:T(8,128)(2,1)} %get-tuple-element.50), channel_id=1, source_target_pairs={{0,4},{2,6},{4,0},{6,2},{1,5},{3,7},{5,1},{7,3},{8,12},{10,14},{12... | collective-permute-start | bytes 1572872 | tf_op jit(solution)/shard_map/ppermute | solution.py:70
  493.7 24.4 %collective-permute-start.52 = (bf16[4,128,512]{2,1,0:T(8,128)(2,1)}, bf16[4,128,512]{2,1,0:T(8,128)(2,1)}, u32[]{:S(2)}, u32[]{:S(2)}) collective-permute-start(bf16[4,128,512]{2,1,0:T(8,128)(2,1)} %get-tuple-element.51), channel_id=1, source_target_pairs={{0,4},{2,6},{4,0},{6,2},{1,5},{3,7},{5,1},{7,3},{8,12},{10,14},{12... | collective-permute-start | bytes 1572872 | tf_op jit(solution)/shard_map/ppermute | solution.py:70
  505.4 20.3 %collective-permute-start.39 = (bf16[4,128,512]{2,1,0:T(8,128)(2,1)S(1)}, bf16[4,128,512]{2,1,0:T(8,128)(2,1)S(1)}, u32[]{:S(2)}, u32[]{:S(2)}) collective-permute-start(bf16[4,128,512]{2,1,0:T(8,128)(2,1)S(1)} %get-tuple-element.53), channel_id=1, source_target_pairs={{0,2},{2,0},{4,6},{6,4},{1,3},{3,1},{5,7},{7,5},{8,10},{10,8},{12,... | collective-permute-start | bytes 1572872 | tf_op jit(solution)/shard_map/ppermute | solution.py:70
  514.9 14.9 %collective-permute-start.42 = (bf16[4,128,512]{2,1,0:T(8,128)(2,1)S(1)}, bf16[4,128,512]{2,1,0:T(8,128)(2,1)S(1)}, u32[]{:S(2)}, u32[]{:S(2)}) collective-permute-start(bf16[4,128,512]{2,1,0:T(8,128)(2,1)S(1)} %get-tuple-element.55), channel_id=1, source_target_pairs={{0,4},{2,6},{4,0},{6,2},{1,5},{3,7},{5,1},{7,3},{8,12},{10,14},{12... | collective-permute-start | bytes 1572872 | tf_op jit(solution)/shard_map/ppermute | solution.py:70
  518.1 21.4 %collective-permute-start.50 = (bf16[4,128,512]{2,1,0:T(8,128)(2,1)S(1)}, bf16[4,128,512]{2,1,0:T(8,128)(2,1)S(1)}, u32[]{:S(2)}, u32[]{:S(2)}) collective-permute-start(bf16[4,128,512]{2,1,0:T(8,128)(2,1)S(1)} %fusion.125), channel_id=1, source_target_pairs={{0,4},{2,6},{4,0},{6,2},{1,5},{3,7},{5,1},{7,3},{8,12},{10,14},{12... | collective-permute-start | bytes 1572872 | tf_op jit(solution)/shard_map/ppermute | solution.py:70
  525.7 42.5 %collective-permute-start.25 = (bf16[512,1024]{1,0:T(8,128)(2,1)S(1)}, bf16[512,1024]{1,0:T(8,128)(2,1)S(1)}, u32[]{:S(2)}, u32[]{:S(2)}) collective-permute-start(bf16[512,1024]{1,0:T(8,128)(2,1)S(1)} %constant_dynamic-slice_fusion.5), channel_id=1, source_target_pairs={{0,1},{1,0},{2,3},{3,2},{4,5},{5,4},{6,7},{7,6},{8,9},{9,8},{10,11... | collective-permute-start | bytes 3145736 | tf_op jit(solution)/shard_map/ppermute | solution.py:44
  529.8 14.9 %collective-permute-start.53 = (bf16[4,128,512]{2,1,0:T(8,128)(2,1)S(1)}, bf16[4,128,512]{2,1,0:T(8,128)(2,1)S(1)}, u32[]{:S(2)}, u32[]{:S(2)}) collective-permute-start(bf16[4,128,512]{2,1,0:T(8,128)(2,1)S(1)} %fusion.123), channel_id=1, source_target_pairs={{0,2},{2,0},{4,6},{6,4},{1,3},{3,1},{5,7},{7,5},{8,10},{10,8},{12,... | collective-permute-start | bytes 1572872 | tf_op jit(solution)/shard_map/ppermute | solution.py:70
  531.9 24.0 %collective-permute-start.38 = (bf16[4,128,512]{2,1,0:T(8,128)(2,1)S(1)}, bf16[4,128,512]{2,1,0:T(8,128)(2,1)S(1)}, u32[]{:S(2)}, u32[]{:S(2)}) collective-permute-start(bf16[4,128,512]{2,1,0:T(8,128)(2,1)S(1)} %get-tuple-element.52), channel_id=1, source_target_pairs={{0,2},{2,0},{4,6},{6,4},{1,3},{3,1},{5,7},{7,5},{8,10},{10,8},{12,... | collective-permute-start | bytes 1572872 | tf_op jit(solution)/shard_map/ppermute | solution.py:70
  539.5 16.3 %collective-permute-start.40 = (bf16[4,128,512]{2,1,0:T(8,128)(2,1)S(1)}, bf16[4,128,512]{2,1,0:T(8,128)(2,1)S(1)}, u32[]{:S(2)}, u32[]{:S(2)}) collective-permute-start(bf16[4,128,512]{2,1,0:T(8,128)(2,1)S(1)} %fusion.129), channel_id=1, source_target_pairs={{0,4},{2,6},{4,0},{6,2},{1,5},{3,7},{5,1},{7,3},{8,12},{10,14},{12... | collective-permute-start | bytes 1572872 | tf_op jit(solution)/shard_map/ppermute | solution.py:70
  542.3 20.9 %collective-permute-start.41 = (bf16[4,128,512]{2,1,0:T(8,128)(2,1)S(1)}, bf16[4,128,512]{2,1,0:T(8,128)(2,1)S(1)}, u32[]{:S(2)}, u32[]{:S(2)}) collective-permute-start(bf16[4,128,512]{2,1,0:T(8,128)(2,1)S(1)} %get-tuple-element.54), channel_id=1, source_target_pairs={{0,4},{2,6},{4,0},{6,2},{1,5},{3,7},{5,1},{7,3},{8,12},{10,14},{12... | collective-permute-start | bytes 1572872 | tf_op jit(solution)/shard_map/ppermute | solution.py:70
  544.6 18.6 %collective-permute-start.43 = (bf16[4,128,512]{2,1,0:T(8,128)(2,1)S(1)}, bf16[4,128,512]{2,1,0:T(8,128)(2,1)S(1)}, u32[]{:S(2)}, u32[]{:S(2)}) collective-permute-start(bf16[4,128,512]{2,1,0:T(8,128)(2,1)S(1)} %fusion.127), channel_id=1, source_target_pairs={{0,2},{2,0},{4,6},{6,4},{1,3},{3,1},{5,7},{7,5},{8,10},{10,8},{12,... | collective-permute-start | bytes 1572872 | tf_op jit(solution)/shard_map/ppermute | solution.py:70
  555.9 14.0 %collective-permute-start.23 = (bf16[512,1024]{1,0:T(8,128)(2,1)S(1)}, bf16[512,1024]{1,0:T(8,128)(2,1)S(1)}, u32[]{:S(2)}, u32[]{:S(2)}) collective-permute-start(bf16[512,1024]{1,0:T(8,128)(2,1)S(1)} %constant_dynamic-slice_fusion.6), channel_id=1, source_target_pairs={{0,1},{1,0},{2,3},{3,2},{4,5},{5,4},{6,7},{7,6},{8,9},{9,8},{10,11... | collective-permute-start | bytes 3145736 | tf_op jit(solution)/shard_map/ppermute | solution.py:44
  555.9 44.0 %collective-permute-start.54 = (bf16[128,512]{1,0:T(8,128)(2,1)}, bf16[128,512]{1,0:T(8,128)(2,1)}, u32[]{:S(2)}, u32[]{:S(2)}) collective-permute-start(bf16[128,512]{1,0:T(8,128)(2,1)} %get-tuple-element.102), channel_id=1, source_target_pairs={{0,24},{8,0},{16,8},{24,16},{1,25},{9,1},{17,9},{25,17},{2,26},{10... | collective-permute-start | bytes 393224 | tf_op jit(solution)/shard_map/ppermute | solution.py:65
  563.2 32.4 %collective-permute-start.56 = (bf16[128,512]{1,0:T(8,128)(2,1)}, bf16[128,512]{1,0:T(8,128)(2,1)}, u32[]{:S(2)}, u32[]{:S(2)}) collective-permute-start(bf16[128,512]{1,0:T(8,128)(2,1)} %get-tuple-element.105), channel_id=1, source_target_pairs={{0,8},{8,16},{16,24},{24,0},{1,9},{9,17},{17,25},{25,1},{2,10},{10... | collective-permute-start | bytes 393224 | tf_op jit(solution)/shard_map/ppermute | solution.py:65
  563.3 37.6 %collective-permute-start.44 = (bf16[128,512]{1,0:T(8,128)(2,1)}, bf16[128,512]{1,0:T(8,128)(2,1)}, u32[]{:S(2)}, u32[]{:S(2)}) collective-permute-start(bf16[128,512]{1,0:T(8,128)(2,1)} %get-tuple-element.106), channel_id=1, source_target_pairs={{0,24},{8,0},{16,8},{24,16},{1,25},{9,1},{17,9},{25,17},{2,26},{10... | collective-permute-start | bytes 393224 | tf_op jit(solution)/shard_map/ppermute | solution.py:65
  568.2 35.1 %collective-permute-start.46 = (bf16[128,512]{1,0:T(8,128)(2,1)}, bf16[128,512]{1,0:T(8,128)(2,1)}, u32[]{:S(2)}, u32[]{:S(2)}) collective-permute-start(bf16[128,512]{1,0:T(8,128)(2,1)} %get-tuple-element.109), channel_id=1, source_target_pairs={{0,8},{8,16},{16,24},{24,0},{1,9},{9,17},{17,25},{25,1},{2,10},{10... | collective-permute-start | bytes 393224 | tf_op jit(solution)/shard_map/ppermute | solution.py:65
  573.6 31.3 %collective-permute-start.26 = (bf16[512,1024]{1,0:T(8,128)(2,1)S(1)}, bf16[512,1024]{1,0:T(8,128)(2,1)}, u32[]{:S(2)}, u32[]{:S(2)}) collective-permute-start(bf16[512,1024]{1,0:T(8,128)(2,1)S(1)} %get-tuple-element.43), channel_id=1, source_target_pairs={{0,1},{1,0},{2,3},{3,2},{4,5},{5,4},{6,7},{7,6},{8,9},{9,8},{10,11... | collective-permute-start | bytes 3145736 | tf_op jit(solution)/shard_map/ppermute | solution.py:44
  590.6 219.2 %all-to-all-start.7 = ((bf16[4,2,65536]{2,1,0:T(2,128)(2,1)}), bf16[4,2,65536]{2,1,0:T(2,128)(2,1)}, u32[]{:S(2)}, u32[]{:S(2)}) async-start(bf16[4,2,65536]{2,1,0:T(2,128)(2,1)} %reshape.685), calls=%async_computation.7 | async-start | bytes 2097152 | tf_op jit(solution)/shard_map/all_to_all | solution.py:160
  595.7 292.7 %all-gather.5.cloned.1.call-start = ((), (), s32[]{:S(2)}) async-start(), calls=%async_computation.18 | async-start | bytes 1486848 | tf_op jit(solution)/shard_map/all_gather | solution.py:430
  597.4 205.4 %collective-permute-start.57 = (bf16[256,512]{1,0:T(8,128)(2,1)}, bf16[256,512]{1,0:T(8,128)(2,1)}, u32[]{:S(2)}, u32[]{:S(2)}) collective-permute-start(bf16[256,512]{1,0:T(8,128)(2,1)} %pad_maximum_fusion.29), channel_id=1, source_target_pairs={{0,8},{8,16},{16,24},{24,0},{1,9},{9,17},{17,25},{25,1},{2,10},{10... | collective-permute-start | bytes 786440 | tf_op jit(solution)/shard_map/ppermute | solution.py:65
  738.2 15.1 %collective-permute-start.29 = (bf16[4,128,512]{2,1,0:T(8,128)(2,1)}, bf16[4,128,512]{2,1,0:T(8,128)(2,1)}, u32[]{:S(2)}, u32[]{:S(2)}) collective-permute-start(bf16[4,128,512]{2,1,0:T(8,128)(2,1)} %get-tuple-element.57), channel_id=1, source_target_pairs={{0,2},{2,0},{4,6},{6,4},{1,3},{3,1},{5,7},{7,5},{8,10},{10,8},{12,... | collective-permute-start | bytes 1572872 | tf_op jit(solution)/shard_map/ppermute | solution.py:70
  739.6 20.4 %collective-permute-start.27 = (bf16[512,1024]{1,0:T(8,128)(2,1)}, bf16[512,1024]{1,0:T(8,128)(2,1)S(1)}, u32[]{:S(2)}, u32[]{:S(2)}) collective-permute-start(bf16[512,1024]{1,0:T(8,128)(2,1)} %constant_dynamic-slice_fusion.4), channel_id=1, source_target_pairs={{0,1},{1,0},{2,3},{3,2},{4,5},{5,4},{6,7},{7,6},{8,9},{9,8},{10,11... | collective-permute-start | bytes 3145736 | tf_op jit(solution)/shard_map/ppermute | solution.py:44
  741.4 15.5 %collective-permute-start.32 = (bf16[4,128,512]{2,1,0:T(8,128)(2,1)}, bf16[4,128,512]{2,1,0:T(8,128)(2,1)}, u32[]{:S(2)}, u32[]{:S(2)}) collective-permute-start(bf16[4,128,512]{2,1,0:T(8,128)(2,1)} %get-tuple-element.59), channel_id=1, source_target_pairs={{0,4},{2,6},{4,0},{6,2},{1,5},{3,7},{5,1},{7,3},{8,12},{10,14},{12... | collective-permute-start | bytes 1572872 | tf_op jit(solution)/shard_map/ppermute | solution.py:70
  746.3 31.3 %collective-permute-start.28 = (bf16[4,128,512]{2,1,0:T(8,128)(2,1)}, bf16[4,128,512]{2,1,0:T(8,128)(2,1)}, u32[]{:S(2)}, u32[]{:S(2)}) collective-permute-start(bf16[4,128,512]{2,1,0:T(8,128)(2,1)} %get-tuple-element.56), channel_id=1, source_target_pairs={{0,2},{2,0},{4,6},{6,4},{1,3},{3,1},{5,7},{7,5},{8,10},{10,8},{12,... | collective-permute-start | bytes 1572872 | tf_op jit(solution)/shard_map/ppermute | solution.py:70
  753.3 19.8 %collective-permute-start.31 = (bf16[4,128,512]{2,1,0:T(8,128)(2,1)}, bf16[4,128,512]{2,1,0:T(8,128)(2,1)}, u32[]{:S(2)}, u32[]{:S(2)}) collective-permute-start(bf16[4,128,512]{2,1,0:T(8,128)(2,1)} %get-tuple-element.58), channel_id=1, source_target_pairs={{0,4},{2,6},{4,0},{6,2},{1,5},{3,7},{5,1},{7,3},{8,12},{10,14},{12... | collective-permute-start | bytes 1572872 | tf_op jit(solution)/shard_map/ppermute | solution.py:70
  756.9 23.5 %collective-permute-start.30 = (bf16[4,128,512]{2,1,0:T(8,128)(2,1)}, bf16[4,128,512]{2,1,0:T(8,128)(2,1)}, u32[]{:S(2)}, u32[]{:S(2)}) collective-permute-start(bf16[4,128,512]{2,1,0:T(8,128)(2,1)} %fusion.133), channel_id=1, source_target_pairs={{0,4},{2,6},{4,0},{6,2},{1,5},{3,7},{5,1},{7,3},{8,12},{10,14},{12... | collective-permute-start | bytes 1572872 | tf_op jit(solution)/shard_map/ppermute | solution.py:70
  760.0 14.9 %collective-permute-start.33 = (bf16[4,128,512]{2,1,0:T(8,128)(2,1)}, bf16[4,128,512]{2,1,0:T(8,128)(2,1)}, u32[]{:S(2)}, u32[]{:S(2)}) collective-permute-start(bf16[4,128,512]{2,1,0:T(8,128)(2,1)} %fusion.131), channel_id=1, source_target_pairs={{0,2},{2,0},{4,6},{6,4},{1,3},{3,1},{5,7},{7,5},{8,10},{10,8},{12,... | collective-permute-start | bytes 1572872 | tf_op jit(solution)/shard_map/ppermute | solution.py:70
  773.1 34.0 %collective-permute-start.55 = (bf16[256,512]{1,0:T(8,128)(2,1)}, bf16[256,512]{1,0:T(8,128)(2,1)S(1)}, u32[]{:S(2)}, u32[]{:S(2)}) collective-permute-start(bf16[256,512]{1,0:T(8,128)(2,1)} %pad_maximum_fusion.28), channel_id=1, source_target_pairs={{0,24},{8,0},{16,8},{24,16},{1,25},{9,1},{17,9},{25,17},{2,26},{10... | collective-permute-start | bytes 786440 | tf_op jit(solution)/shard_map/ppermute | solution.py:65
  775.0 34.0 %collective-permute-start.47 = (bf16[256,512]{1,0:T(8,128)(2,1)}, bf16[256,512]{1,0:T(8,128)(2,1)S(1)}, u32[]{:S(2)}, u32[]{:S(2)}) collective-permute-start(bf16[256,512]{1,0:T(8,128)(2,1)} %pad_maximum_fusion.27), channel_id=1, source_target_pairs={{0,8},{8,16},{16,24},{24,0},{1,9},{9,17},{17,25},{25,1},{2,10},{10... | collective-permute-start | bytes 786440 | tf_op jit(solution)/shard_map/ppermute | solution.py:65
  777.6 31.4 %collective-permute-start.45 = (bf16[256,512]{1,0:T(8,128)(2,1)}, bf16[256,512]{1,0:T(8,128)(2,1)S(1)}, u32[]{:S(2)}, u32[]{:S(2)}) collective-permute-start(bf16[256,512]{1,0:T(8,128)(2,1)} %pad_maximum_fusion.26), channel_id=1, source_target_pairs={{0,24},{8,0},{16,8},{24,16},{1,25},{9,1},{17,9},{25,17},{2,26},{10... | collective-permute-start | bytes 786440 | tf_op jit(solution)/shard_map/ppermute | solution.py:65
  780.5 16.3 %collective-permute-start.36 = (bf16[128,512]{1,0:T(8,128)(2,1)S(1)}, bf16[128,512]{1,0:T(8,128)(2,1)S(1)}, u32[]{:S(2)}, u32[]{:S(2)}) collective-permute-start(bf16[128,512]{1,0:T(8,128)(2,1)S(1)} %get-tuple-element.113), channel_id=1, source_target_pairs={{0,8},{8,16},{16,24},{24,0},{1,9},{9,17},{17,25},{25,1},{2,10},{10... | collective-permute-start | bytes 393224 | tf_op jit(solution)/shard_map/ppermute | solution.py:65
  802.1 29.1 %collective-permute-start.37 = (bf16[256,512]{1,0:T(8,128)(2,1)}, bf16[256,512]{1,0:T(8,128)(2,1)}, u32[]{:S(2)}, u32[]{:S(2)}) collective-permute-start(bf16[256,512]{1,0:T(8,128)(2,1)} %pad_maximum_fusion.25), channel_id=1, source_target_pairs={{0,8},{8,16},{16,24},{24,0},{1,9},{9,17},{17,25},{25,1},{2,10},{10... | collective-permute-start | bytes 786440 | tf_op jit(solution)/shard_map/ppermute | solution.py:65
  802.8 28.3 %collective-permute-start.35 = (bf16[256,512]{1,0:T(8,128)(2,1)}, bf16[256,512]{1,0:T(8,128)(2,1)}, u32[]{:S(2)}, u32[]{:S(2)}) collective-permute-start(bf16[256,512]{1,0:T(8,128)(2,1)} %pad_maximum_fusion.24), channel_id=1, source_target_pairs={{0,24},{8,0},{16,8},{24,16},{1,25},{9,1},{17,9},{25,17},{2,26},{10... | collective-permute-start | bytes 786440 | tf_op jit(solution)/shard_map/ppermute | solution.py:65
  809.8 22.8 %all-to-all-start.16 = ((bf16[512,2,128]{0,2,1:T(8,128)(2,1)}), bf16[512,2,128]{0,2,1:T(8,128)(2,1)}, u32[]{:S(2)}, u32[]{:S(2)}) async-start(bf16[512,2,128]{0,2,1:T(8,128)(2,1)} %bitcast.215), calls=%async_computation.16 | async-start | bytes 524288 | tf_op jit(solution)/shard_map/all_to_all | solution.py:147
  850.4 29.8 %all-to-all-start.11 = ((bf16[4,2,65536]{2,1,0:T(2,128)(2,1)}), bf16[4,2,65536]{2,1,0:T(2,128)(2,1)S(1)}, u32[]{:S(2)}, u32[]{:S(2)}) async-start(bf16[4,2,65536]{2,1,0:T(2,128)(2,1)} %reshape.687), calls=%async_computation.11 | async-start | bytes 2097152 | tf_op jit(solution)/shard_map/all_to_all | solution.py:160
  (145 other events, 1811.8 us)
Sparse Core Ops, SparseCore 0:
  44.4 122.0 all-reduce.5
  172.4 53.5 all-reduce.3
  773.2 58.0 all-gather.4

commit v2 on v1

--- a/solution.py
+++ b/solution.py
@@ -286,7 +286,8 @@
             condition.reshape(-1),
         ]
     )
-    smalls = lax.all_gather(small, ("narrow", "col", "core"))
+    small = jnp.pad(small, (0, -small.shape[0] % 1024)).reshape(-1, 128)
+    smalls = lax.all_gather(small, ("narrow", "col", "core")).reshape(n_size * w_size, -1)
     part = b_proj.shape[0]
 
     def full_bias(low, count):
@@ -308,7 +309,9 @@
     qv_rows = turned(qv_rows, 1).reshape(2, -1).astype(jnp.float32)
     qkv_bias = jnp.concatenate([qv_rows[0], jnp.zeros_like(qv_rows[0]), qv_rows[1]])
 
-    cond_all = smalls[:w_size, 10 * part + fc1_size :].reshape(-1, feature_count)
+    cond_all = smalls[
+        :w_size, 10 * part + fc1_size : 10 * part + fc1_size + condition.size
+    ].reshape(-1, feature_count)
     cond_act_all = jax.nn.silu(cond_all.astype(jnp.float32)).astype(jnp.bfloat16)
     cond_cols = lax.dynamic_slice_in_dim(cond_act_all, wide * rows_low, rows_low, 1)
     mod_part = jnp.einsum("sd,dcn->scn", cond_cols, w_ada, preferred_element_type=jnp.float32)

time: 957 us -> 871 us (0.910)
  waiting for transfers between devices: 305 us -> 185 us
  blocking collectives: 68 us -> 122 us
  local copies, waits for them, and re-layouts: 149 us -> 136 us
    unnamed x4 -> x2, waiting for transfers between devices: 119 us -> 0.03 us
    all_gather x0 -> x1, blocking collectives: none -> 54.2 us  [per_device(): lax.all_gather(small, ('narrow', 'col', 'core'))]
    unnamed x306 -> x317, local copies, waits for them, and re-layouts: 36.1 us -> 33.5 us
  transfers between devices with their start and end apart: 72 -> 71, of which waited for: 23 -> 22; matrix products, arithmetic and copies ran while one was open for 38% -> 40% of each run, Pallas kernels for 0% -> 0%
where the time goes in v2:
time: 871 us; the launch traced here: 859 us
  waiting for transfers between devices  185 us (21%)
  matrix products  147 us (17%)
  local copies, waits for them, and re-layouts  136 us (16%)
  other arithmetic  136 us (16%)
  blocking collectives  122 us (14%)
  starting transfers between devices  117 us (13%)
  between operations  16.8 us (2%)
    ppermute x30, waiting for transfers between devices, flip_col(): return lax.ppermute(values, 'col', [(i, i ^ bit) for i in range(size)])  67.4 us
    all_gather x1, blocking collectives, per_device(): lax.all_gather(small, ('narrow', 'col', 'core'))  54.2 us
    all_gather x1, blocking collectives, per_device(): cond_parts = lax.all_gather(cond_part, ('narrow', 'col', 'core'))  40.4 us
    all_to_all x2, waiting for transfers between devices, to_images(): lax.all_to_all(shaped.reshape(2 * seq_count, half, width), 'narrow', 0, 2...  36.8 us
    ppermute x20, starting transfers between devices, shift_narrow(): lax.ppermute(values, 'narrow', [(i, (i + step) % size) for i in range(siz...  36.3 us
    psum x1, waiting for transfers between devices, per_device(): mod_total = lax.psum(mod_part, ('col', 'core'))  35.8 us
    convert_element_type x8, other arithmetic, attend_back(): grad_scores = (soft_float * (grad_soft - inner)).astype(jnp.bfloat16)  35.8 us
    ppermute x30, starting transfers between devices, flip_col(): return lax.ppermute(values, 'col', [(i, i ^ bit) for i in range(size)])  35.7 us
  transfers between devices with their start and end apart: 71, of which 22 were waited for; matrix products, arithmetic and copies ran while one was open for 40% of the time, Pallas kernels for 0%

profile of v2, /device:TPU:0, one launch (start us, length us, event | category | flops | bytes accessed | tf_op | source)
XLA Modules:
  0.0 859.3 jit_solution(17253810126678588592)
XLA Ops:
  7.2 3.4 all-to-all-start.4
  12.4 3.4 all-to-all-start.3
  23.1 3.4 all-to-all-start.6
  28.1 3.4 all-to-all-start.5
  34.2 3.8 collective-permute-start.15
  38.3 54.2 %all_gather.15 = bf16[32,24,128]{2,1,0:T(8,128)(2,1)S(1)} all-gather(bf16[1,24,128]{2,1,0:T(8,128)(2,1)S(1)} %pad_bitcast_fusion), channel_id=1, replica_groups=mesh['narrow'=4,'col'=4,'core'=2] {'narrow','col','core'}, dimensions={0}, use_global_device_ids=true | all-gather | bytes 202752 | tf_op jit(solution)/shard_map/all_gather | solution.py:290
  97.3 3.9 collective-permute-start.4
  101.8 3.6 collective-permute-done.2
  107.4 35.8 %all-reduce.3.cloned.1.call-done = f32[16,6,256]{2,0,1:T(8,128)} async-done(((f32[16,6,256]{2,0,1:T(8,128)}), f32[16,6,256]{2,0,1:T(8,128)}) %all-reduce.3.cloned.1.call-update) | async-done | bytes 98320 | tf_op jit(solution)/shard_map/psum | solution.py:318
  144.6 4.6 all-to-all-start.2
  161.4 4.4 all-to-all-start
  175.1 6.8 collective-permute-done.5
  186.7 6.3 collective-permute-done.8
  195.1 9.2 %collective-permute-done.10 = bf16[4,128,512]{2,1,0:T(8,128)(2,1)S(1)} collective-permute-done((bf16[4,128,512]{2,1,0:T(8,128)(2,1)}, bf16[4,128,512]{2,1,0:T(8,128)(2,1)S(1)}, u32[]{:S(2)}, u32[]{:S(2)}) %collective-permute-start.10) | collective-permute-done | bytes 524320 | tf_op jit(solution)/shard_map/ppermute | solution.py:70
  212.7 5.4 all_to_all.237
  218.1 3.5 all-to-all-start.1
  230.2 17.7 %all-to-all-done.1 = bf16[4,512,256]{2,1,0:T(8,128)(2,1)S(1)} async-done(((bf16[4,512,256]{2,1,0:T(8,128)(2,1)}), bf16[4,512,256]{2,1,0:T(8,128)(2,1)S(1)}, u32[]{:S(2)}, u32[]{:S(2)}) %all-to-all-start.1) | async-done | bytes 1048608 | tf_op jit(solution)/shard_map/all_to_all | solution.py:153
  247.9 4.8 all-to-all-start.10
  259.1 19.1 %all-to-all-done.10 = bf16[4,512,256]{2,1,0:T(8,128)(2,1)} async-done(((bf16[4,512,256]{2,1,0:T(8,128)(2,1)}), bf16[4,512,256]{2,1,0:T(8,128)(2,1)}, u32[]{:S(2)}, u32[]{:S(2)}) %all-to-all-start.10) | async-done | bytes 1048608 | tf_op jit(solution)/shard_map/all_to_all | solution.py:153
  287.4 7.2 add_convert_fusion
  340.3 3.2 copy.245
  345.7 4.5 fusion.55
  350.3 6.6 convolution_convert_fusion.5
  356.9 12.1 %convert_reduce_fusion = (f32[2048]{0:T(1024)S(1)}, bf16[1024,2048]{1,0:T(8,128)(2,1)}) fusion(f32[1024,2048]{1,0:T(8,128)S(1)} %fusion.55, f32[2048]{0:T(1024)S(1)} %bitcast.620, bf16[1024,2048]{1,0:T(8,128)(2,1)S(1)} %bitcast.539, bf16[512,1024]{1,0:T(8,128)(2,1)S(1)} %copy-done.81, bf16[512,1024]{1,0:T(8,128)(2,1)S(1)} %get-tuple-element.64), kind=kOutput, calls=%fused_computation.14 | convolution fusion | flops 4345296896 | bytes 18890752 | tf_op jit(solution)/shard_map/dot_general | solution.py:351
  369.0 6.7 convolution_convert_fusion.1
  375.7 5.9 convolution_convert_fusion.4
  381.6 6.1 convolution_convert_fusion.2
  389.1 7.8 reshape.588
  407.8 8.0 reshape.585
  421.6 7.3 collective-permute-done.49
  434.4 5.4 collective-permute-done.39
  439.9 3.9 collective-permute-done.42
  446.1 7.5 collective-permute-done.50
  461.6 8.3 collective-permute-done.38
  472.4 4.9 collective-permute-done.41
  477.3 3.9 collective-permute-start.44
  483.9 3.7 multiply_reduce_fusion.16
  487.6 4.6 copy.246
  492.8 8.0 reduce.13
  500.8 3.8 reshape.686
  504.6 5.1 all-to-all-start.7
  549.7 4.6 multiply_convert_fusion.8
  556.9 3.3 multiply_convert_fusion.1
  560.2 4.7 multiply_convert_fusion.2
  564.8 4.7 multiply_convert_fusion.3
  569.5 4.6 multiply_convert_fusion.4
  574.1 4.6 multiply_convert_fusion.5
  578.7 4.7 multiply_convert_fusion.6
  583.4 4.6 multiply_convert_fusion.7
  627.6 6.9 convolution_convert_fusion.3
  634.5 5.0 convolution_convert_fusion
  661.8 5.6 collective-permute-done.29
  696.3 14.5 %collective-permute-done.36 = bf16[128,512]{1,0:T(8,128)(2,1)S(1)} collective-permute-done((bf16[128,512]{1,0:T(8,128)(2,1)S(1)}, bf16[128,512]{1,0:T(8,128)(2,1)S(1)}, u32[]{:S(2)}, u32[]{:S(2)}) %collective-permute-start.36) | collective-permute-done | bytes 131104 | tf_op jit(solution)/shard_map/ppermute | solution.py:65
  717.0 4.3 collective-permute-start.35
  723.9 4.3 all-to-all-start.16
  736.2 7.0 reduce.14
  746.8 4.7 all_to_all.238
  751.5 4.6 all_to_all.239
  756.0 4.6 all_to_all.240
  760.6 3.9 all_to_all.241
  764.6 3.5 all-to-all-start.11
  774.2 20.1 %all-to-all-done.11 = bf16[4,2,65536]{2,1,0:T(2,128)(2,1)S(1)} async-done(((bf16[4,2,65536]{2,1,0:T(2,128)(2,1)}), bf16[4,2,65536]{2,1,0:T(2,128)(2,1)S(1)}, u32[]{:S(2)}, u32[]{:S(2)}) %all-to-all-start.11) | async-done | bytes 1048608 | tf_op jit(solution)/shard_map/all_to_all | solution.py:160
  796.2 4.8 all_to_all.242
  810.7 40.4 %all-gather.1 = f32[512,128]{1,0:T(8,128)S(1)} all-gather(f32[16,128]{1,0:T(8,128)S(1)} %convolution_bitcast_fusion), channel_id=3, replica_groups=mesh['narrow'=4,'col'=4,'core'=2] {'narrow','col','core'}, dimensions={0}, use_global_device_ids=true | all-gather | bytes 270336 | tf_op jit(solution)/shard_map/all_gather | solution.py:457
  (716 shorter events, 341.2 us)
Async XLA Ops:
  17.9 79.3 %collective-permute-start.1 = (bf16[256,512]{1,0:T(8,128)(2,1)S(1)}, bf16[256,512]{1,0:T(8,128)(2,1)S(1)}, u32[]{:S(2)}, u32[]{:S(2)}) collective-permute-start(bf16[256,512]{1,0:T(8,128)(2,1)S(1)} %get-tuple-element.153), channel_id=1, source_target_pairs={{0,8},{8,16},{16,24},{24,0},{1,9},{9,17},{17,25},{25,1},{2,10},{10... | collective-permute-start | bytes 786440 | tf_op jit(solution)/shard_map/ppermute | solution.py:65
  21.0 76.3 %collective-permute-start.3 = (bf16[256,512]{1,0:T(8,128)(2,1)S(1)}, bf16[256,512]{1,0:T(8,128)(2,1)S(1)}, u32[]{:S(2)}, u32[]{:S(2)}) collective-permute-start(bf16[256,512]{1,0:T(8,128)(2,1)S(1)} %get-tuple-element.153), channel_id=1, source_target_pairs={{0,24},{8,0},{16,8},{24,16},{1,25},{9,1},{17,9},{25,17},{2,26},{10... | collective-permute-start | bytes 786440 | tf_op jit(solution)/shard_map/ppermute | solution.py:65
  31.5 111.6 %all-reduce.3.cloned.1.call-start = ((), (), s32[]{:S(2)}) async-start(), calls=%async_computation.17 | async-start | bytes 196608 | tf_op jit(solution)/shard_map/psum | solution.py:318
  34.2 115.0 %collective-permute-start.13 = (bf16[256,1024]{1,0:T(8,128)(2,1)}, bf16[256,1024]{1,0:T(8,128)(2,1)S(1)}, u32[]{:S(2)}, u32[]{:S(2)}) collective-permute-start(bf16[256,1024]{1,0:T(8,128)(2,1)} %get-tuple-element.115), channel_id=1, source_target_pairs={{0,8},{8,16},{16,24},{24,0},{1,9},{9,17},{17,25},{25,1},{2,10},{10... | collective-permute-start | bytes 1572872 | tf_op jit(solution)/shard_map/ppermute | solution.py:65
  34.2 117.7 %collective-permute-start.15 = (bf16[256,1024]{1,0:T(8,128)(2,1)}, bf16[256,1024]{1,0:T(8,128)(2,1)S(1)}, u32[]{:S(2)}, u32[]{:S(2)}) collective-permute-start(bf16[256,1024]{1,0:T(8,128)(2,1)} %get-tuple-element.115), channel_id=1, source_target_pairs={{0,24},{8,0},{16,8},{24,16},{1,25},{9,1},{17,9},{25,17},{2,26},{10... | collective-permute-start | bytes 1572872 | tf_op jit(solution)/shard_map/ppermute | solution.py:65
  107.3 64.8 %collective-permute-start.9 = (bf16[4,128,512]{2,1,0:T(8,128)(2,1)}, bf16[4,128,512]{2,1,0:T(8,128)(2,1)}, u32[]{:S(2)}, u32[]{:S(2)}) collective-permute-start(bf16[4,128,512]{2,1,0:T(8,128)(2,1)} %get-tuple-element.100), channel_id=1, source_target_pairs={{0,4},{2,6},{4,0},{6,2},{1,5},{3,7},{5,1},{7,3},{8,12},{10,14},{12... | collective-permute-start | bytes 1572872 | tf_op jit(solution)/shard_map/ppermute | solution.py:70
  144.6 16.8 %all-to-all-start.2 = ((f32[4,6,256]{2,1,0:T(8,128)}), f32[4,6,256]{2,1,0:T(8,128)}, u32[]{:S(2)}, u32[]{:S(2)}) async-start(f32[4,6,256]{2,1,0:T(8,128)} %copy.226), calls=%async_computation.2 | async-start | bytes 65536 | tf_op jit(solution)/shard_map/all_to_all | solution.py:320
  149.9 20.2 %collective-permute-start.14 = (bf16[128,1024]{1,0:T(8,128)(2,1)}, bf16[128,1024]{1,0:T(8,128)(2,1)}, u32[]{:S(2)}, u32[]{:S(2)}) collective-permute-start(bf16[128,1024]{1,0:T(8,128)(2,1)} %slice.660), channel_id=1, source_target_pairs={{0,8},{8,16},{16,24},{24,0},{1,9},{9,17},{17,25},{25,1},{2,10},{10... | collective-permute-start | bytes 786440 | tf_op jit(solution)/shard_map/ppermute | solution.py:65
  152.7 20.0 %collective-permute-start.16 = (bf16[128,1024]{1,0:T(8,128)(2,1)}, bf16[128,1024]{1,0:T(8,128)(2,1)}, u32[]{:S(2)}, u32[]{:S(2)}) collective-permute-start(bf16[128,1024]{1,0:T(8,128)(2,1)} %slice.661), channel_id=1, source_target_pairs={{0,24},{8,0},{16,8},{24,16},{1,25},{9,1},{17,9},{25,17},{2,26},{10... | collective-permute-start | bytes 786440 | tf_op jit(solution)/shard_map/ppermute | solution.py:65
  161.4 51.3 %all-to-all-start = ((bf16[2,2,512,256]{3,2,0,1:T(8,128)(2,1)}), bf16[2,2,512,256]{3,2,0,1:T(8,128)(2,1)}, u32[]{:S(2)}, u32[]{:S(2)}) async-start(bf16[2,2,512,256]{3,2,0,1:T(8,128)(2,1)} %copy.224), calls=%async_computation | async-start | bytes 2097152 | tf_op jit(solution)/shard_map/all_to_all | solution.py:147
  166.7 15.3 %collective-permute-start.5 = (bf16[4,128,512]{2,1,0:T(8,128)(2,1)}, bf16[4,128,512]{2,1,0:T(8,128)(2,1)}, u32[]{:S(2)}, u32[]{:S(2)}) collective-permute-start(bf16[4,128,512]{2,1,0:T(8,128)(2,1)} %get-tuple-element.101), channel_id=1, source_target_pairs={{0,2},{2,0},{4,6},{6,4},{1,3},{3,1},{5,7},{7,5},{8,10},{10,8},{12,... | collective-permute-start | bytes 1572872 | tf_op jit(solution)/shard_map/ppermute | solution.py:70
  170.0 23.0 %collective-permute-start.8 = (bf16[4,128,512]{2,1,0:T(8,128)(2,1)}, bf16[4,128,512]{2,1,0:T(8,128)(2,1)S(1)}, u32[]{:S(2)}, u32[]{:S(2)}) collective-permute-start(bf16[4,128,512]{2,1,0:T(8,128)(2,1)} %get-tuple-element.100), channel_id=1, source_target_pairs={{0,2},{2,0},{4,6},{6,4},{1,3},{3,1},{5,7},{7,5},{8,10},{10,8},{12,... | collective-permute-start | bytes 1572872 | tf_op jit(solution)/shard_map/ppermute | solution.py:70
  170.0 39.0 %collective-permute-start.6 = (bf16[4,128,512]{2,1,0:T(8,128)(2,1)}, bf16[4,128,512]{2,1,0:T(8,128)(2,1)S(1)}, u32[]{:S(2)}, u32[]{:S(2)}) collective-permute-start(bf16[4,128,512]{2,1,0:T(8,128)(2,1)} %get-tuple-element.101), channel_id=1, source_target_pairs={{0,4},{2,6},{4,0},{6,2},{1,5},{3,7},{5,1},{7,3},{8,12},{10,14},{12... | collective-permute-start | bytes 1572872 | tf_op jit(solution)/shard_map/ppermute | solution.py:70
  172.1 32.2 %collective-permute-start.10 = (bf16[4,128,512]{2,1,0:T(8,128)(2,1)}, bf16[4,128,512]{2,1,0:T(8,128)(2,1)S(1)}, u32[]{:S(2)}, u32[]{:S(2)}) collective-permute-start(bf16[4,128,512]{2,1,0:T(8,128)(2,1)} %collective-permute-done.9), channel_id=1, source_target_pairs={{0,2},{2,0},{4,6},{6,4},{1,3},{3,1},{5,7},{7,5},{8,10},{10,8},{12,... | collective-permute-start | bytes 1572872 | tf_op jit(solution)/shard_map/ppermute | solution.py:70
  181.9 27.8 %collective-permute-start.7 = (bf16[4,128,512]{2,1,0:T(8,128)(2,1)}, bf16[4,128,512]{2,1,0:T(8,128)(2,1)S(1)}, u32[]{:S(2)}, u32[]{:S(2)}) collective-permute-start(bf16[4,128,512]{2,1,0:T(8,128)(2,1)} %collective-permute-done.5), channel_id=1, source_target_pairs={{0,4},{2,6},{4,0},{6,2},{1,5},{3,7},{5,1},{7,3},{8,12},{10,14},{12... | collective-permute-start | bytes 1572872 | tf_op jit(solution)/shard_map/ppermute | solution.py:70
  186.2 140.4 %collective-permute-start.20 = (bf16[4,128,1024]{2,1,0:T(8,128)(2,1)}, bf16[4,128,1024]{2,1,0:T(8,128)(2,1)}, u32[]{:S(2)}, u32[]{:S(2)}) collective-permute-start(bf16[4,128,1024]{2,1,0:T(8,128)(2,1)} %get-tuple-element.82), channel_id=1, source_target_pairs={{0,2},{2,0},{4,6},{6,4},{1,3},{3,1},{5,7},{7,5},{8,10},{10,8},{12,... | collective-permute-start | bytes 3145736 | tf_op jit(solution)/shard_map/ppermute | solution.py:70
  193.0 90.8 %collective-permute-start.21 = (bf16[4,128,1024]{2,1,0:T(8,128)(2,1)}, bf16[4,128,1024]{2,1,0:T(8,128)(2,1)}, u32[]{:S(2)}, u32[]{:S(2)}) collective-permute-start(bf16[4,128,1024]{2,1,0:T(8,128)(2,1)} %get-tuple-element.82), channel_id=1, source_target_pairs={{0,4},{2,6},{4,0},{6,2},{1,5},{3,7},{5,1},{7,3},{8,12},{10,14},{12... | collective-permute-start | bytes 3145736 | tf_op jit(solution)/shard_map/ppermute | solution.py:70
  204.3 79.6 %collective-permute-start.17 = (bf16[4,128,1024]{2,1,0:T(8,128)(2,1)}, bf16[4,128,1024]{2,1,0:T(8,128)(2,1)}, u32[]{:S(2)}, u32[]{:S(2)}) collective-permute-start(bf16[4,128,1024]{2,1,0:T(8,128)(2,1)} %get-tuple-element.83), channel_id=1, source_target_pairs={{0,2},{2,0},{4,6},{6,4},{1,3},{3,1},{5,7},{7,5},{8,10},{10,8},{12,... | collective-permute-start | bytes 3145736 | tf_op jit(solution)/shard_map/ppermute | solution.py:70
  209.1 119.7 %collective-permute-start.18 = (bf16[4,128,1024]{2,1,0:T(8,128)(2,1)}, bf16[4,128,1024]{2,1,0:T(8,128)(2,1)}, u32[]{:S(2)}, u32[]{:S(2)}) collective-permute-start(bf16[4,128,1024]{2,1,0:T(8,128)(2,1)} %get-tuple-element.83), channel_id=1, source_target_pairs={{0,4},{2,6},{4,0},{6,2},{1,5},{3,7},{5,1},{7,3},{8,12},{10,14},{12... | collective-permute-start | bytes 3145736 | tf_op jit(solution)/shard_map/ppermute | solution.py:70
  218.1 29.8 %all-to-all-start.1 = ((bf16[4,512,256]{2,1,0:T(8,128)(2,1)}), bf16[4,512,256]{2,1,0:T(8,128)(2,1)S(1)}, u32[]{:S(2)}, u32[]{:S(2)}) async-start(bf16[4,512,256]{2,1,0:T(8,128)(2,1)} %bitcast.3), calls=%async_computation.1 | async-start | bytes 2097152 | tf_op jit(solution)/shard_map/all_to_all | solution.py:153
  247.9 30.3 %all-to-all-start.10 = ((bf16[4,512,256]{2,1,0:T(8,128)(2,1)}), bf16[4,512,256]{2,1,0:T(8,128)(2,1)}, u32[]{:S(2)}, u32[]{:S(2)}) async-start(bf16[4,512,256]{2,1,0:T(8,128)(2,1)} %bitcast.131), calls=%async_computation.10 | async-start | bytes 2097152 | tf_op jit(solution)/shard_map/all_to_all | solution.py:153
  257.9 27.6 %collective-permute-start = (bf16[512,1024]{1,0:T(8,128)(2,1)}, bf16[512,1024]{1,0:T(8,128)(2,1)}, u32[]{:S(2)}, u32[]{:S(2)}) collective-permute-start(bf16[512,1024]{1,0:T(8,128)(2,1)} %add_convert_fusion.4), channel_id=1, source_target_pairs={{0,1},{1,0},{2,3},{3,2},{4,5},{5,4},{6,7},{7,6},{8,9},{9,8},{10,11... | collective-permute-start | bytes 3145736 | tf_op jit(solution)/shard_map/ppermute | solution.py:44
  283.8 40.0 %collective-permute-start.24 = (bf16[512,1024]{1,0:T(8,128)(2,1)S(1)}, bf16[512,1024]{1,0:T(8,128)(2,1)}, u32[]{:S(2)}, u32[]{:S(2)}) collective-permute-start(bf16[512,1024]{1,0:T(8,128)(2,1)S(1)} %multiply_convert_fusion.10), channel_id=1, source_target_pairs={{0,1},{1,0},{2,3},{3,2},{4,5},{5,4},{6,7},{7,6},{8,9},{9,8},{10,11... | collective-permute-start | bytes 3145736 | tf_op jit(solution)/shard_map/ppermute | solution.py:44
  283.9 42.7 %collective-permute-start.22 = (bf16[4,128,1024]{2,1,0:T(8,128)(2,1)}, bf16[4,128,1024]{2,1,0:T(8,128)(2,1)}, u32[]{:S(2)}, u32[]{:S(2)}) collective-permute-start(bf16[4,128,1024]{2,1,0:T(8,128)(2,1)} %collective-permute-done.21), channel_id=1, source_target_pairs={{0,2},{2,0},{4,6},{6,4},{1,3},{3,1},{5,7},{7,5},{8,10},{10,8},{12,... | collective-permute-start | bytes 3145736 | tf_op jit(solution)/shard_map/ppermute | solution.py:70
  285.4 43.4 %collective-permute-start.19 = (bf16[4,128,1024]{2,1,0:T(8,128)(2,1)}, bf16[4,128,1024]{2,1,0:T(8,128)(2,1)}, u32[]{:S(2)}, u32[]{:S(2)}) collective-permute-start(bf16[4,128,1024]{2,1,0:T(8,128)(2,1)} %collective-permute-done.17), channel_id=1, source_target_pairs={{0,4},{2,6},{4,0},{6,2},{1,5},{3,7},{5,1},{7,3},{8,12},{10,14},{12... | collective-permute-start | bytes 3145736 | tf_op jit(solution)/shard_map/ppermute | solution.py:70
  323.8 8.8 %collective-permute-start.11 = (bf16[512,1024]{1,0:T(8,128)(2,1)S(1)}, bf16[512,1024]{1,0:T(8,128)(2,1)S(1)}, u32[]{:S(2)}, u32[]{:S(2)}) collective-permute-start(bf16[512,1024]{1,0:T(8,128)(2,1)S(1)} %constant_dynamic-slice_fusion.8), channel_id=1, source_target_pairs={{0,1},{1,0},{2,3},{3,2},{4,5},{5,4},{6,7},{7,6},{8,9},{9,8},{10,11... | collective-permute-start | bytes 3145736 | tf_op jit(solution)/shard_map/ppermute | solution.py:44
  334.0 11.0 %collective-permute-start.12 = (bf16[512,1024]{1,0:T(8,128)(2,1)S(1)}, bf16[512,1024]{1,0:T(8,128)(2,1)S(1)}, u32[]{:S(2)}, u32[]{:S(2)}) collective-permute-start(bf16[512,1024]{1,0:T(8,128)(2,1)S(1)} %add_convert_fusion.3), channel_id=1, source_target_pairs={{0,1},{1,0},{2,3},{3,2},{4,5},{5,4},{6,7},{7,6},{8,9},{9,8},{10,11... | collective-permute-start | bytes 3145736 | tf_op jit(solution)/shard_map/ppermute | solution.py:44
  402.7 43.2 %collective-permute-start.48 = (bf16[4,128,512]{2,1,0:T(8,128)(2,1)}, bf16[4,128,512]{2,1,0:T(8,128)(2,1)S(1)}, u32[]{:S(2)}, u32[]{:S(2)}) collective-permute-start(bf16[4,128,512]{2,1,0:T(8,128)(2,1)} %get-tuple-element.48), channel_id=1, source_target_pairs={{0,2},{2,0},{4,6},{6,4},{1,3},{3,1},{5,7},{7,5},{8,10},{10,8},{12,... | collective-permute-start | bytes 1572872 | tf_op jit(solution)/shard_map/ppermute | solution.py:70
  404.6 24.3 %collective-permute-start.49 = (bf16[4,128,512]{2,1,0:T(8,128)(2,1)}, bf16[4,128,512]{2,1,0:T(8,128)(2,1)}, u32[]{:S(2)}, u32[]{:S(2)}) collective-permute-start(bf16[4,128,512]{2,1,0:T(8,128)(2,1)} %get-tuple-element.49), channel_id=1, source_target_pairs={{0,2},{2,0},{4,6},{6,4},{1,3},{3,1},{5,7},{7,5},{8,10},{10,8},{12,... | collective-permute-start | bytes 1572872 | tf_op jit(solution)/shard_map/ppermute | solution.py:70
  405.8 50.5 %collective-permute-start.51 = (bf16[4,128,512]{2,1,0:T(8,128)(2,1)}, bf16[4,128,512]{2,1,0:T(8,128)(2,1)S(1)}, u32[]{:S(2)}, u32[]{:S(2)}) collective-permute-start(bf16[4,128,512]{2,1,0:T(8,128)(2,1)} %get-tuple-element.50), channel_id=1, source_target_pairs={{0,4},{2,6},{4,0},{6,2},{1,5},{3,7},{5,1},{7,3},{8,12},{10,14},{12... | collective-permute-start | bytes 1572872 | tf_op jit(solution)/shard_map/ppermute | solution.py:70
  407.8 24.4 %collective-permute-start.52 = (bf16[4,128,512]{2,1,0:T(8,128)(2,1)}, bf16[4,128,512]{2,1,0:T(8,128)(2,1)}, u32[]{:S(2)}, u32[]{:S(2)}) collective-permute-start(bf16[4,128,512]{2,1,0:T(8,128)(2,1)} %get-tuple-element.51), channel_id=1, source_target_pairs={{0,4},{2,6},{4,0},{6,2},{1,5},{3,7},{5,1},{7,3},{8,12},{10,14},{12... | collective-permute-start | bytes 1572872 | tf_op jit(solution)/shard_map/ppermute | solution.py:70
  419.4 20.3 %collective-permute-start.39 = (bf16[4,128,512]{2,1,0:T(8,128)(2,1)S(1)}, bf16[4,128,512]{2,1,0:T(8,128)(2,1)S(1)}, u32[]{:S(2)}, u32[]{:S(2)}) collective-permute-start(bf16[4,128,512]{2,1,0:T(8,128)(2,1)S(1)} %get-tuple-element.53), channel_id=1, source_target_pairs={{0,2},{2,0},{4,6},{6,4},{1,3},{3,1},{5,7},{7,5},{8,10},{10,8},{12,... | collective-permute-start | bytes 1572872 | tf_op jit(solution)/shard_map/ppermute | solution.py:70
  429.0 14.9 %collective-permute-start.42 = (bf16[4,128,512]{2,1,0:T(8,128)(2,1)S(1)}, bf16[4,128,512]{2,1,0:T(8,128)(2,1)S(1)}, u32[]{:S(2)}, u32[]{:S(2)}) collective-permute-start(bf16[4,128,512]{2,1,0:T(8,128)(2,1)S(1)} %get-tuple-element.55), channel_id=1, source_target_pairs={{0,4},{2,6},{4,0},{6,2},{1,5},{3,7},{5,1},{7,3},{8,12},{10,14},{12... | collective-permute-start | bytes 1572872 | tf_op jit(solution)/shard_map/ppermute | solution.py:70
  432.2 21.4 %collective-permute-start.50 = (bf16[4,128,512]{2,1,0:T(8,128)(2,1)S(1)}, bf16[4,128,512]{2,1,0:T(8,128)(2,1)S(1)}, u32[]{:S(2)}, u32[]{:S(2)}) collective-permute-start(bf16[4,128,512]{2,1,0:T(8,128)(2,1)S(1)} %fusion.125), channel_id=1, source_target_pairs={{0,4},{2,6},{4,0},{6,2},{1,5},{3,7},{5,1},{7,3},{8,12},{10,14},{12... | collective-permute-start | bytes 1572872 | tf_op jit(solution)/shard_map/ppermute | solution.py:70
  439.7 42.4 %collective-permute-start.25 = (bf16[512,1024]{1,0:T(8,128)(2,1)S(1)}, bf16[512,1024]{1,0:T(8,128)(2,1)S(1)}, u32[]{:S(2)}, u32[]{:S(2)}) collective-permute-start(bf16[512,1024]{1,0:T(8,128)(2,1)S(1)} %constant_dynamic-slice_fusion.5), channel_id=1, source_target_pairs={{0,1},{1,0},{2,3},{3,2},{4,5},{5,4},{6,7},{7,6},{8,9},{9,8},{10,11... | collective-permute-start | bytes 3145736 | tf_op jit(solution)/shard_map/ppermute | solution.py:44
  443.8 14.9 %collective-permute-start.53 = (bf16[4,128,512]{2,1,0:T(8,128)(2,1)S(1)}, bf16[4,128,512]{2,1,0:T(8,128)(2,1)S(1)}, u32[]{:S(2)}, u32[]{:S(2)}) collective-permute-start(bf16[4,128,512]{2,1,0:T(8,128)(2,1)S(1)} %fusion.123), channel_id=1, source_target_pairs={{0,2},{2,0},{4,6},{6,4},{1,3},{3,1},{5,7},{7,5},{8,10},{10,8},{12,... | collective-permute-start | bytes 1572872 | tf_op jit(solution)/shard_map/ppermute | solution.py:70
  445.9 24.0 %collective-permute-start.38 = (bf16[4,128,512]{2,1,0:T(8,128)(2,1)S(1)}, bf16[4,128,512]{2,1,0:T(8,128)(2,1)S(1)}, u32[]{:S(2)}, u32[]{:S(2)}) collective-permute-start(bf16[4,128,512]{2,1,0:T(8,128)(2,1)S(1)} %get-tuple-element.52), channel_id=1, source_target_pairs={{0,2},{2,0},{4,6},{6,4},{1,3},{3,1},{5,7},{7,5},{8,10},{10,8},{12,... | collective-permute-start | bytes 1572872 | tf_op jit(solution)/shard_map/ppermute | solution.py:70
  453.6 16.4 %collective-permute-start.40 = (bf16[4,128,512]{2,1,0:T(8,128)(2,1)S(1)}, bf16[4,128,512]{2,1,0:T(8,128)(2,1)S(1)}, u32[]{:S(2)}, u32[]{:S(2)}) collective-permute-start(bf16[4,128,512]{2,1,0:T(8,128)(2,1)S(1)} %fusion.129), channel_id=1, source_target_pairs={{0,4},{2,6},{4,0},{6,2},{1,5},{3,7},{5,1},{7,3},{8,12},{10,14},{12... | collective-permute-start | bytes 1572872 | tf_op jit(solution)/shard_map/ppermute | solution.py:70
  456.3 21.0 %collective-permute-start.41 = (bf16[4,128,512]{2,1,0:T(8,128)(2,1)S(1)}, bf16[4,128,512]{2,1,0:T(8,128)(2,1)S(1)}, u32[]{:S(2)}, u32[]{:S(2)}) collective-permute-start(bf16[4,128,512]{2,1,0:T(8,128)(2,1)S(1)} %get-tuple-element.54), channel_id=1, source_target_pairs={{0,4},{2,6},{4,0},{6,2},{1,5},{3,7},{5,1},{7,3},{8,12},{10,14},{12... | collective-permute-start | bytes 1572872 | tf_op jit(solution)/shard_map/ppermute | solution.py:70
  458.7 18.6 %collective-permute-start.43 = (bf16[4,128,512]{2,1,0:T(8,128)(2,1)S(1)}, bf16[4,128,512]{2,1,0:T(8,128)(2,1)S(1)}, u32[]{:S(2)}, u32[]{:S(2)}) collective-permute-start(bf16[4,128,512]{2,1,0:T(8,128)(2,1)S(1)} %fusion.127), channel_id=1, source_target_pairs={{0,2},{2,0},{4,6},{6,4},{1,3},{3,1},{5,7},{7,5},{8,10},{10,8},{12,... | collective-permute-start | bytes 1572872 | tf_op jit(solution)/shard_map/ppermute | solution.py:70
  469.9 13.9 %collective-permute-start.23 = (bf16[512,1024]{1,0:T(8,128)(2,1)S(1)}, bf16[512,1024]{1,0:T(8,128)(2,1)S(1)}, u32[]{:S(2)}, u32[]{:S(2)}) collective-permute-start(bf16[512,1024]{1,0:T(8,128)(2,1)S(1)} %constant_dynamic-slice_fusion.6), channel_id=1, source_target_pairs={{0,1},{1,0},{2,3},{3,2},{4,5},{5,4},{6,7},{7,6},{8,9},{9,8},{10,11... | collective-permute-start | bytes 3145736 | tf_op jit(solution)/shard_map/ppermute | solution.py:44
  469.9 43.9 %collective-permute-start.54 = (bf16[128,512]{1,0:T(8,128)(2,1)}, bf16[128,512]{1,0:T(8,128)(2,1)}, u32[]{:S(2)}, u32[]{:S(2)}) collective-permute-start(bf16[128,512]{1,0:T(8,128)(2,1)} %get-tuple-element.102), channel_id=1, source_target_pairs={{0,24},{8,0},{16,8},{24,16},{1,25},{9,1},{17,9},{25,17},{2,26},{10... | collective-permute-start | bytes 393224 | tf_op jit(solution)/shard_map/ppermute | solution.py:65
  477.2 32.4 %collective-permute-start.56 = (bf16[128,512]{1,0:T(8,128)(2,1)}, bf16[128,512]{1,0:T(8,128)(2,1)}, u32[]{:S(2)}, u32[]{:S(2)}) collective-permute-start(bf16[128,512]{1,0:T(8,128)(2,1)} %get-tuple-element.105), channel_id=1, source_target_pairs={{0,8},{8,16},{16,24},{24,0},{1,9},{9,17},{17,25},{25,1},{2,10},{10... | collective-permute-start | bytes 393224 | tf_op jit(solution)/shard_map/ppermute | solution.py:65
  477.3 37.5 %collective-permute-start.44 = (bf16[128,512]{1,0:T(8,128)(2,1)}, bf16[128,512]{1,0:T(8,128)(2,1)}, u32[]{:S(2)}, u32[]{:S(2)}) collective-permute-start(bf16[128,512]{1,0:T(8,128)(2,1)} %get-tuple-element.106), channel_id=1, source_target_pairs={{0,24},{8,0},{16,8},{24,16},{1,25},{9,1},{17,9},{25,17},{2,26},{10... | collective-permute-start | bytes 393224 | tf_op jit(solution)/shard_map/ppermute | solution.py:65
  482.2 35.2 %collective-permute-start.46 = (bf16[128,512]{1,0:T(8,128)(2,1)}, bf16[128,512]{1,0:T(8,128)(2,1)}, u32[]{:S(2)}, u32[]{:S(2)}) collective-permute-start(bf16[128,512]{1,0:T(8,128)(2,1)} %get-tuple-element.109), channel_id=1, source_target_pairs={{0,8},{8,16},{16,24},{24,0},{1,9},{9,17},{17,25},{25,1},{2,10},{10... | collective-permute-start | bytes 393224 | tf_op jit(solution)/shard_map/ppermute | solution.py:65
  487.6 31.4 %collective-permute-start.26 = (bf16[512,1024]{1,0:T(8,128)(2,1)S(1)}, bf16[512,1024]{1,0:T(8,128)(2,1)}, u32[]{:S(2)}, u32[]{:S(2)}) collective-permute-start(bf16[512,1024]{1,0:T(8,128)(2,1)S(1)} %get-tuple-element.43), channel_id=1, source_target_pairs={{0,1},{1,0},{2,3},{3,2},{4,5},{5,4},{6,7},{7,6},{8,9},{9,8},{10,11... | collective-permute-start | bytes 3145736 | tf_op jit(solution)/shard_map/ppermute | solution.py:44
  504.6 219.4 %all-to-all-start.7 = ((bf16[4,2,65536]{2,1,0:T(2,128)(2,1)}), bf16[4,2,65536]{2,1,0:T(2,128)(2,1)}, u32[]{:S(2)}, u32[]{:S(2)}) async-start(bf16[4,2,65536]{2,1,0:T(2,128)(2,1)} %reshape.686), calls=%async_computation.7 | async-start | bytes 2097152 | tf_op jit(solution)/shard_map/all_to_all | solution.py:160
  509.7 292.9 %all-gather.4.cloned.1.call-start = ((), (), s32[]{:S(2)}) async-start(), calls=%async_computation.18 | async-start | bytes 1486848 | tf_op jit(solution)/shard_map/all_gather | solution.py:433
  511.4 205.6 %collective-permute-start.57 = (bf16[256,512]{1,0:T(8,128)(2,1)}, bf16[256,512]{1,0:T(8,128)(2,1)}, u32[]{:S(2)}, u32[]{:S(2)}) collective-permute-start(bf16[256,512]{1,0:T(8,128)(2,1)} %pad_maximum_fusion.29), channel_id=1, source_target_pairs={{0,8},{8,16},{16,24},{24,0},{1,9},{9,17},{17,25},{25,1},{2,10},{10... | collective-permute-start | bytes 786440 | tf_op jit(solution)/shard_map/ppermute | solution.py:65
  652.2 15.2 %collective-permute-start.29 = (bf16[4,128,512]{2,1,0:T(8,128)(2,1)}, bf16[4,128,512]{2,1,0:T(8,128)(2,1)}, u32[]{:S(2)}, u32[]{:S(2)}) collective-permute-start(bf16[4,128,512]{2,1,0:T(8,128)(2,1)} %get-tuple-element.57), channel_id=1, source_target_pairs={{0,2},{2,0},{4,6},{6,4},{1,3},{3,1},{5,7},{7,5},{8,10},{10,8},{12,... | collective-permute-start | bytes 1572872 | tf_op jit(solution)/shard_map/ppermute | solution.py:70
  653.7 20.4 %collective-permute-start.27 = (bf16[512,1024]{1,0:T(8,128)(2,1)}, bf16[512,1024]{1,0:T(8,128)(2,1)S(1)}, u32[]{:S(2)}, u32[]{:S(2)}) collective-permute-start(bf16[512,1024]{1,0:T(8,128)(2,1)} %constant_dynamic-slice_fusion.4), channel_id=1, source_target_pairs={{0,1},{1,0},{2,3},{3,2},{4,5},{5,4},{6,7},{7,6},{8,9},{9,8},{10,11... | collective-permute-start | bytes 3145736 | tf_op jit(solution)/shard_map/ppermute | solution.py:44
  655.5 15.5 %collective-permute-start.32 = (bf16[4,128,512]{2,1,0:T(8,128)(2,1)}, bf16[4,128,512]{2,1,0:T(8,128)(2,1)}, u32[]{:S(2)}, u32[]{:S(2)}) collective-permute-start(bf16[4,128,512]{2,1,0:T(8,128)(2,1)} %get-tuple-element.59), channel_id=1, source_target_pairs={{0,4},{2,6},{4,0},{6,2},{1,5},{3,7},{5,1},{7,3},{8,12},{10,14},{12... | collective-permute-start | bytes 1572872 | tf_op jit(solution)/shard_map/ppermute | solution.py:70
  660.4 31.1 %collective-permute-start.28 = (bf16[4,128,512]{2,1,0:T(8,128)(2,1)}, bf16[4,128,512]{2,1,0:T(8,128)(2,1)}, u32[]{:S(2)}, u32[]{:S(2)}) collective-permute-start(bf16[4,128,512]{2,1,0:T(8,128)(2,1)} %get-tuple-element.56), channel_id=1, source_target_pairs={{0,2},{2,0},{4,6},{6,4},{1,3},{3,1},{5,7},{7,5},{8,10},{10,8},{12,... | collective-permute-start | bytes 1572872 | tf_op jit(solution)/shard_map/ppermute | solution.py:70
  667.4 20.0 %collective-permute-start.31 = (bf16[4,128,512]{2,1,0:T(8,128)(2,1)}, bf16[4,128,512]{2,1,0:T(8,128)(2,1)}, u32[]{:S(2)}, u32[]{:S(2)}) collective-permute-start(bf16[4,128,512]{2,1,0:T(8,128)(2,1)} %get-tuple-element.58), channel_id=1, source_target_pairs={{0,4},{2,6},{4,0},{6,2},{1,5},{3,7},{5,1},{7,3},{8,12},{10,14},{12... | collective-permute-start | bytes 1572872 | tf_op jit(solution)/shard_map/ppermute | solution.py:70
  671.0 23.6 %collective-permute-start.30 = (bf16[4,128,512]{2,1,0:T(8,128)(2,1)}, bf16[4,128,512]{2,1,0:T(8,128)(2,1)}, u32[]{:S(2)}, u32[]{:S(2)}) collective-permute-start(bf16[4,128,512]{2,1,0:T(8,128)(2,1)} %fusion.133), channel_id=1, source_target_pairs={{0,4},{2,6},{4,0},{6,2},{1,5},{3,7},{5,1},{7,3},{8,12},{10,14},{12... | collective-permute-start | bytes 1572872 | tf_op jit(solution)/shard_map/ppermute | solution.py:70
  674.1 15.1 %collective-permute-start.33 = (bf16[4,128,512]{2,1,0:T(8,128)(2,1)}, bf16[4,128,512]{2,1,0:T(8,128)(2,1)}, u32[]{:S(2)}, u32[]{:S(2)}) collective-permute-start(bf16[4,128,512]{2,1,0:T(8,128)(2,1)} %fusion.131), channel_id=1, source_target_pairs={{0,2},{2,0},{4,6},{6,4},{1,3},{3,1},{5,7},{7,5},{8,10},{10,8},{12,... | collective-permute-start | bytes 1572872 | tf_op jit(solution)/shard_map/ppermute | solution.py:70
  687.4 34.0 %collective-permute-start.55 = (bf16[256,512]{1,0:T(8,128)(2,1)}, bf16[256,512]{1,0:T(8,128)(2,1)S(1)}, u32[]{:S(2)}, u32[]{:S(2)}) collective-permute-start(bf16[256,512]{1,0:T(8,128)(2,1)} %pad_maximum_fusion.28), channel_id=1, source_target_pairs={{0,24},{8,0},{16,8},{24,16},{1,25},{9,1},{17,9},{25,17},{2,26},{10... | collective-permute-start | bytes 786440 | tf_op jit(solution)/shard_map/ppermute | solution.py:65
  689.1 34.0 %collective-permute-start.47 = (bf16[256,512]{1,0:T(8,128)(2,1)}, bf16[256,512]{1,0:T(8,128)(2,1)S(1)}, u32[]{:S(2)}, u32[]{:S(2)}) collective-permute-start(bf16[256,512]{1,0:T(8,128)(2,1)} %pad_maximum_fusion.27), channel_id=1, source_target_pairs={{0,8},{8,16},{16,24},{24,0},{1,9},{9,17},{17,25},{25,1},{2,10},{10... | collective-permute-start | bytes 786440 | tf_op jit(solution)/shard_map/ppermute | solution.py:65
  691.6 31.5 %collective-permute-start.45 = (bf16[256,512]{1,0:T(8,128)(2,1)}, bf16[256,512]{1,0:T(8,128)(2,1)S(1)}, u32[]{:S(2)}, u32[]{:S(2)}) collective-permute-start(bf16[256,512]{1,0:T(8,128)(2,1)} %pad_maximum_fusion.26), channel_id=1, source_target_pairs={{0,24},{8,0},{16,8},{24,16},{1,25},{9,1},{17,9},{25,17},{2,26},{10... | collective-permute-start | bytes 786440 | tf_op jit(solution)/shard_map/ppermute | solution.py:65
  694.6 16.2 %collective-permute-start.36 = (bf16[128,512]{1,0:T(8,128)(2,1)S(1)}, bf16[128,512]{1,0:T(8,128)(2,1)S(1)}, u32[]{:S(2)}, u32[]{:S(2)}) collective-permute-start(bf16[128,512]{1,0:T(8,128)(2,1)S(1)} %get-tuple-element.113), channel_id=1, source_target_pairs={{0,8},{8,16},{16,24},{24,0},{1,9},{9,17},{17,25},{25,1},{2,10},{10... | collective-permute-start | bytes 393224 | tf_op jit(solution)/shard_map/ppermute | solution.py:65
  716.2 29.1 %collective-permute-start.37 = (bf16[256,512]{1,0:T(8,128)(2,1)}, bf16[256,512]{1,0:T(8,128)(2,1)}, u32[]{:S(2)}, u32[]{:S(2)}) collective-permute-start(bf16[256,512]{1,0:T(8,128)(2,1)} %pad_maximum_fusion.25), channel_id=1, source_target_pairs={{0,8},{8,16},{16,24},{24,0},{1,9},{9,17},{17,25},{25,1},{2,10},{10... | collective-permute-start | bytes 786440 | tf_op jit(solution)/shard_map/ppermute | solution.py:65
  717.0 28.3 %collective-permute-start.35 = (bf16[256,512]{1,0:T(8,128)(2,1)}, bf16[256,512]{1,0:T(8,128)(2,1)}, u32[]{:S(2)}, u32[]{:S(2)}) collective-permute-start(bf16[256,512]{1,0:T(8,128)(2,1)} %pad_maximum_fusion.24), channel_id=1, source_target_pairs={{0,24},{8,0},{16,8},{24,16},{1,25},{9,1},{17,9},{25,17},{2,26},{10... | collective-permute-start | bytes 786440 | tf_op jit(solution)/shard_map/ppermute | solution.py:65
  723.9 22.9 %all-to-all-start.16 = ((bf16[512,2,128]{0,2,1:T(8,128)(2,1)}), bf16[512,2,128]{0,2,1:T(8,128)(2,1)}, u32[]{:S(2)}, u32[]{:S(2)}) async-start(bf16[512,2,128]{0,2,1:T(8,128)(2,1)} %bitcast.216), calls=%async_computation.16 | async-start | bytes 524288 | tf_op jit(solution)/shard_map/all_to_all | solution.py:147
  764.6 29.8 %all-to-all-start.11 = ((bf16[4,2,65536]{2,1,0:T(2,128)(2,1)}), bf16[4,2,65536]{2,1,0:T(2,128)(2,1)S(1)}, u32[]{:S(2)}, u32[]{:S(2)}) async-start(bf16[4,2,65536]{2,1,0:T(2,128)(2,1)} %reshape.688), calls=%async_computation.11 | async-start | bytes 2097152 | tf_op jit(solution)/shard_map/all_to_all | solution.py:160
  (150 other events, 1791.8 us)
Sparse Core Ops, SparseCore 0:
  93.6 49.4 all-reduce.2
  687.5 59.0 all-gather.3
